TPU v7x, 512 devices: a whole 4x8x8 slice. The times are simulated.
512 devices in a mesh: lon: 64 (over z_hi, y, x), lat: 8 (over z_lo, core).
Axes of the slice: x: 4, y: 8, z: 8 (z_hi: 2, z_lo: 4; z = z_hi * 4 + z_lo), core: 2. Of those that a mesh axis runs over, the one named last changes fastest.
Arguments:
- state: bfloat16 [128, 256, 512], P('lat', 'lon'), may hold values from -6 to 6
- conv_weight: bfloat16 [4608, 512], P('lon'), may hold values from -0.09375 to 0.09375
- conv_bias: float32 [512], replicated, may hold values from -5 to 5
- w_qkv: bfloat16 [512, 1536], replicated, may hold values from -0.5 to 0.5
- w_out: bfloat16 [512, 512], replicated, may hold values from -0.25 to 0.25
- cotangent: bfloat16 [128, 256, 512], P('lat', 'lon'), may hold values from -6 to 6
Outputs:
- state_grad: bfloat16 [128, 256, 512], P('lat', 'lon')
All inputs are finite; a program needn't handle non-finite values.
Results may differ from a plain program's by a relative error of at most 0.029.
Values may be sent and summed in bfloat16 or wider, within the bound.
A program may use at most 64 MiB of HBM per device.

v0:
```python
import math

import jax
import jax.numpy as jnp
from jax import lax
from jax.sharding import PartitionSpec as P

HEAD_DIM = 128


softcap = 20.0


def extended_2(shard, sides, width):
    for axis, dim in sides:
        devices, length = (lax.axis_size(axis), shard.shape[dim])
        up = [(i, (i + 1) % devices) for i in range(devices)]
        down = [(j, i) for i, j in up]
        last = lax.slice_in_dim(shard, length - width, length, axis=dim)
        initial = lax.slice_in_dim(shard, 0, width, axis=dim)
        before = lax.ppermute(last, axis, up)
        after = lax.ppermute(initial, axis, down)
        shard = jnp.concatenate([before, shard, after], axis=dim)
    return shard


def attend_rows(parts):
    queries, key_rows, value_rows, out_grad = parts
    inv_root = 1.0 / math.sqrt(queries.shape[-1])
    raw = (
        jnp.einsum("gnid,gnjd->gnij", queries, key_rows, preferred_element_type=jnp.float32)
        * inv_root
    )
    scores = softcap * jnp.tanh(raw / softcap)
    expo = jnp.exp(scores)
    probs = expo / jnp.sum(expo, axis=-1, keepdims=True)
    probs_b = probs.astype(jnp.bfloat16)
    attended = jnp.einsum(
        "gnij,gnjd->gnid", probs_b, value_rows, preferred_element_type=jnp.float32
    ).astype(jnp.bfloat16)
    centre = jnp.sum(
        out_grad.astype(jnp.float32) * attended.astype(jnp.float32), axis=-1, keepdims=True
    )
    dprobs = jnp.einsum("gnid,gnjd->gnij", out_grad, value_rows, preferred_element_type=jnp.float32)
    score_grad = (
        probs * (dprobs - centre) * (1.0 - jnp.square(scores / softcap)) * inv_root
    ).astype(jnp.bfloat16)
    grad_query = jnp.einsum(
        "gnij,gnjd->gnid", score_grad, key_rows, preferred_element_type=jnp.float32
    ).astype(jnp.bfloat16)
    grad_key = jnp.einsum(
        "gnij,gnid->gnjd", score_grad, queries, preferred_element_type=jnp.float32
    ).astype(jnp.bfloat16)
    grad_value = jnp.einsum(
        "gnij,gnid->gnjd", probs_b, out_grad, preferred_element_type=jnp.float32
    ).astype(jnp.bfloat16)
    return (
        lax.all_to_all(grad_query, "lon", split_axis=2, concat_axis=0, tiled=True),
        lax.all_to_all(grad_key, "lon", split_axis=2, concat_axis=0, tiled=True),
        lax.all_to_all(grad_value, "lon", split_axis=2, concat_axis=0, tiled=True),
    )


def body(state, conv_weight, conv_bias, w_qkv, w_out, cotangent):
    lat_rows, lon_cols, channels = state.shape
    head_dim = HEAD_DIM
    n_heads = channels // head_dim
    cell_count = lat_rows * lon_cols
    groups = lax.axis_size("lon")
    per_group = lat_rows * n_heads // groups
    lat_place = lax.axis_index("lat")
    lat_last = lax.axis_size("lat") - 1
    row_keep = jnp.concatenate(
        [
            (lat_place > 0).astype(jnp.bfloat16)[None],
            jnp.ones((lat_rows,), jnp.bfloat16),
            (lat_place < lat_last).astype(jnp.bfloat16)[None],
        ]
    )

    def with_rims(field):
        extended = extended_2(field, (("lon", 1), ("lat", 0)), 1)
        return extended * row_keep[:, None, None]

    extended_state = with_rims(state)
    windows = [
        extended_state[row_off : row_off + lat_rows, col_off : col_off + lon_cols]
        for row_off in range(3)
        for col_off in range(3)
    ]
    patches = jnp.concatenate(windows, axis=-1).reshape(cell_count, 9 * channels)
    preact = jnp.dot(
        patches,
        lax.all_gather(conv_weight, "lon", axis=0, tiled=True),
        preferred_element_type=jnp.float32,
    )
    preact = preact + conv_bias
    sigmoid_pre = jax.nn.sigmoid(preact)
    activated = (preact * sigmoid_pre).astype(jnp.bfloat16).reshape(lat_rows, lon_cols, channels)
    qkv_weight = w_qkv.reshape(channels, 3, n_heads, head_dim)
    projected = jnp.einsum(
        "rlc,cthd->trhld", activated, qkv_weight, preferred_element_type=jnp.float32
    ).astype(jnp.bfloat16)
    out_grad = jnp.einsum(
        "rlc,hdc->rhld",
        cotangent,
        w_out.reshape(n_heads, head_dim, channels),
        preferred_element_type=jnp.float32,
    ).astype(jnp.bfloat16)
    layout = (groups, per_group, lon_cols, head_dim)
    grad_query, grad_key, grad_value = attend_rows(
        (
            lax.all_to_all(
                projected[0].reshape(layout), "lon", split_axis=0, concat_axis=2, tiled=True
            ),
            lax.all_to_all(
                projected[1].reshape(layout), "lon", split_axis=0, concat_axis=2, tiled=True
            ),
            lax.all_to_all(
                projected[2].reshape(layout), "lon", split_axis=0, concat_axis=2, tiled=True
            ),
            lax.all_to_all(
                out_grad.reshape(layout), "lon", split_axis=0, concat_axis=2, tiled=True
            ),
        )
    )
    back_shape = (lat_rows, n_heads, lon_cols, head_dim)
    grad_act = cotangent.astype(jnp.float32)
    for grad_part, column_set in ((grad_query, 0), (grad_key, 1), (grad_value, 2)):
        grad_act = grad_act + jnp.einsum(
            "rhld,chd->rlc",
            grad_part.reshape(back_shape),
            qkv_weight[:, column_set],
            preferred_element_type=jnp.float32,
        )
    grad_pre = (
        grad_act.reshape(cell_count, channels) * sigmoid_pre * (1.0 + preact * (1.0 - sigmoid_pre))
    ).astype(jnp.bfloat16)
    extended_grad = with_rims(grad_pre.reshape(lat_rows, lon_cols, channels))
    flat_grad = extended_grad.reshape((lat_rows + 2) * (lon_cols + 2), channels)
    tap_grad = jnp.einsum(
        "ec,nc->en",
        flat_grad,
        lax.all_gather(conv_weight, "lon", axis=0, tiled=True),
        preferred_element_type=jnp.float32,
    )
    tap_grad = tap_grad.reshape(lat_rows + 2, lon_cols + 2, 9, channels)
    result = jnp.zeros((lat_rows, lon_cols, channels), jnp.float32)
    for row_off in range(3):
        for col_off in range(3):
            result = (
                result
                + tap_grad[
                    2 - row_off : 2 - row_off + lat_rows,
                    2 - col_off : 2 - col_off + lon_cols,
                    3 * row_off + col_off,
                ]
            )
    return result.astype(jnp.bfloat16)


def solution(mesh):
    return jax.shard_map(
        body,
        mesh=mesh,
        in_specs=(P("lat", "lon", None), P("lon", None), P(), P(), P(), P("lat", "lon", None)),
        out_specs=P("lat", "lon", None),
        check_vma=False,
    )
```

profile of v0, /device:TPU:62, one launch (start us, length us, event | category | flops | bytes accessed | tf_op | source)
XLA Modules:
  0.0 343.1 jit_solution(7248987732911959145)
XLA Ops:
  6.5 0.7 all-gather.2.cloned.1.call-update
  7.3 1.0 fusion.42
  8.2 10.0 %collective-permute-start = (bf16[16,1,512]{2,1,0:T(2,128)(2,1)S(1)}, bf16[16,1,512]{2,1,0:T(2,128)(2,1)S(1)}, u32[]{:S(2)}, u32[]{:S(2)}) collective-permute-start(bf16[16,1,512]{2,1,0:T(2,128)(2,1)S(1)} %get-tuple-element.14), channel_id=1, source_target_pairs={{0,8},{8,16},{16,24},{24,32},{32,40},{40,48},{48,56},{56,64},{64,7... | collective-permute-start | bytes 49160 | tf_op jit(solution)/shard_map/ppermute | solution.py:21
  18.3 1.9 collective-permute-start.1
  20.2 1.1 fusion.15
  21.3 0.1 copy.87
  21.4 0.7 copy.88
  22.1 13.1 %all-to-all-start.2 = ((bf16[64,1,4,128]{3,2,1,0:T(4,128)(2,1)}), bf16[64,1,4,128]{3,2,1,0:T(4,128)(2,1)S(1)}, u32[]{:S(2)}, u32[]{:S(2)}) async-start(bf16[64,1,4,128]{3,2,1,0:T(4,128)(2,1)} %copy.88), calls=%async_computation.2 | async-start | bytes 131072 | tf_op jit(solution)/shard_map/all_to_all | solution.py:122
  35.2 0.7 pad_maximum_fusion.5
  35.9 1.9 collective-permute-start.2
  37.9 5.4 %collective-permute-start.3 = (bf16[1,6,512]{2,1,0:T(8,128)(2,1)S(1)}, bf16[1,6,512]{2,1,0:T(8,128)(2,1)S(1)}, u32[]{:S(2)}, u32[]{:S(2)}) collective-permute-start(bf16[1,6,512]{2,1,0:T(8,128)(2,1)S(1)} %get-tuple-element.11), channel_id=1, source_target_pairs={{1,0},{2,1},{3,2},{4,3},{5,4},{6,5},{7,6},{0,7},{9,8},{10,9},{11,1... | collective-permute-start | bytes 18440 | tf_op jit(solution)/shard_map/ppermute | solution.py:22
  43.3 0.1 pad_maximum_fusion.6
  43.4 1.7 copy.79
  45.2 0.1 maximum_multiply_fusion
  45.8 0.1 reshape.164
  45.9 131.8 %all-gather.2.cloned.1.call-done = bf16[4608,512]{1,0:T(8,128)(2,1)} async-done(((bf16[72,512]{1,0:T(8,128)(2,1)}), bf16[4608,512]{1,0:T(8,128)(2,1)}) %all-gather.2.cloned.1.call-update) | async-done | bytes 4718608 | tf_op jit(solution)/shard_map/all_gather | solution.py:94
  177.7 3.3 multiply_convert_fusion.1
  181.0 0.6 fusion.5
  181.6 0.7 copy.85
  182.3 8.7 %all-to-all-start.1 = ((bf16[64,1,4,128]{3,2,1,0:T(4,128)(2,1)}), bf16[64,1,4,128]{3,2,1,0:T(4,128)(2,1)S(1)}, u32[]{:S(2)}, u32[]{:S(2)}) async-start(bf16[64,1,4,128]{3,2,1,0:T(4,128)(2,1)} %copy.85), calls=%async_computation.1 | async-start | bytes 131072 | tf_op jit(solution)/shard_map/all_to_all | solution.py:116
  191.1 0.7 copy.83
  191.7 9.9 %all-to-all-done.1 = bf16[64,1,4,128]{3,2,1,0:T(4,128)(2,1)S(1)} async-done(((bf16[64,1,4,128]{3,2,1,0:T(4,128)(2,1)}), bf16[64,1,4,128]{3,2,1,0:T(4,128)(2,1)S(1)}, u32[]{:S(2)}, u32[]{:S(2)}) %all-to-all-start.1) | async-done | bytes 65568 | tf_op jit(solution)/shard_map/all_to_all | solution.py:116
  201.6 8.7 %all-to-all-start = ((bf16[64,1,4,128]{3,2,1,0:T(4,128)(2,1)}), bf16[64,1,4,128]{3,2,1,0:T(4,128)(2,1)S(1)}, u32[]{:S(2)}, u32[]{:S(2)}) async-start(bf16[64,1,4,128]{3,2,1,0:T(4,128)(2,1)} %copy.83), calls=%async_computation | async-start | bytes 131072 | tf_op jit(solution)/shard_map/all_to_all | solution.py:113
  210.3 0.1 copy.91
  210.5 0.7 copy.90
  211.1 9.8 %all-to-all-done = bf16[64,1,4,128]{3,2,1,0:T(4,128)(2,1)S(1)} async-done(((bf16[64,1,4,128]{3,2,1,0:T(4,128)(2,1)}), bf16[64,1,4,128]{3,2,1,0:T(4,128)(2,1)S(1)}, u32[]{:S(2)}, u32[]{:S(2)}) %all-to-all-start) | async-done | bytes 65568 | tf_op jit(solution)/shard_map/all_to_all | solution.py:113
  220.9 8.7 %all-to-all-start.3 = ((bf16[64,1,4,128]{3,2,1,0:T(4,128)(2,1)}), bf16[64,1,4,128]{3,2,1,0:T(4,128)(2,1)S(1)}, u32[]{:S(2)}, u32[]{:S(2)}) async-start(bf16[64,1,4,128]{3,2,1,0:T(4,128)(2,1)} %copy.90), calls=%async_computation.3 | async-start | bytes 131072 | tf_op jit(solution)/shard_map/all_to_all | solution.py:119
  229.6 0.2 fusion.17
  229.9 10.3 %all-to-all-done.3 = bf16[64,1,4,128]{3,2,1,0:T(4,128)(2,1)S(1)} async-done(((bf16[64,1,4,128]{3,2,1,0:T(4,128)(2,1)}), bf16[64,1,4,128]{3,2,1,0:T(4,128)(2,1)S(1)}, u32[]{:S(2)}, u32[]{:S(2)}) %all-to-all-start.3) | async-done | bytes 65568 | tf_op jit(solution)/shard_map/all_to_all | solution.py:119
  240.2 0.2 fusion.11
  240.4 0.2 fusion.4
  240.6 0.2 fusion.12
  240.9 0.1 copy.138
  241.0 0.6 broadcast.49
  241.5 1.0 reduce.6
  242.6 0.7 reshape.201
  243.3 8.7 %all-to-all-start.4 = ((bf16[64,2,256]{2,1,0:T(2,128)(2,1)}), bf16[64,2,256]{2,1,0:T(2,128)(2,1)S(1)}, u32[]{:S(2)}, u32[]{:S(2)}) async-start(bf16[64,2,256]{2,1,0:T(2,128)(2,1)} %reshape.201), calls=%async_computation.4 | async-start | bytes 131072 | tf_op jit(solution)/shard_map/all_to_all | solution.py:58
  252.0 0.2 fusion.13
  252.1 0.1 copy.137
  252.2 1.0 reduce.5
  253.3 0.7 reshape.199
  254.0 8.6 %all-to-all-done.4 = bf16[64,2,256]{2,1,0:T(2,128)(2,1)S(1)} async-done(((bf16[64,2,256]{2,1,0:T(2,128)(2,1)}), bf16[64,2,256]{2,1,0:T(2,128)(2,1)S(1)}, u32[]{:S(2)}, u32[]{:S(2)}) %all-to-all-start.4) | async-done | bytes 65568 | tf_op jit(solution)/shard_map/all_to_all | solution.py:58
  262.6 8.7 %all-to-all-start.5 = ((bf16[64,2,256]{2,1,0:T(2,128)(2,1)}), bf16[64,2,256]{2,1,0:T(2,128)(2,1)S(1)}, u32[]{:S(2)}, u32[]{:S(2)}) async-start(bf16[64,2,256]{2,1,0:T(2,128)(2,1)} %reshape.199), calls=%async_computation.5 | async-start | bytes 131072 | tf_op jit(solution)/shard_map/all_to_all | solution.py:59
  271.2 0.2 fusion.14
  271.4 0.1 copy.136
  271.5 1.1 reduce.4
  272.6 0.7 reshape.197
  273.3 8.6 %all-to-all-done.5 = bf16[64,2,256]{2,1,0:T(2,128)(2,1)S(1)} async-done(((bf16[64,2,256]{2,1,0:T(2,128)(2,1)}), bf16[64,2,256]{2,1,0:T(2,128)(2,1)S(1)}, u32[]{:S(2)}, u32[]{:S(2)}) %all-to-all-start.5) | async-done | bytes 65568 | tf_op jit(solution)/shard_map/all_to_all | solution.py:59
  281.8 8.9 %all-to-all-start.6 = ((bf16[64,2,256]{2,1,0:T(2,128)(2,1)}), bf16[64,2,256]{2,1,0:T(2,128)(2,1)S(1)}, u32[]{:S(2)}, u32[]{:S(2)}) async-start(bf16[64,2,256]{2,1,0:T(2,128)(2,1)} %reshape.197), calls=%async_computation.6 | async-start | bytes 131072 | tf_op jit(solution)/shard_map/all_to_all | solution.py:60
  290.8 0.1 reshape.200
  290.9 10.4 %all-to-all-done.6 = bf16[64,2,256]{2,1,0:T(2,128)(2,1)S(1)} async-done(((bf16[64,2,256]{2,1,0:T(2,128)(2,1)}), bf16[64,2,256]{2,1,0:T(2,128)(2,1)S(1)}, u32[]{:S(2)}, u32[]{:S(2)}) %all-to-all-start.6) | async-done | bytes 65568 | tf_op jit(solution)/shard_map/all_to_all | solution.py:60
  301.4 0.2 convolution_bitcast_fusion.1
  301.6 0.2 convolution_bitcast_fusion
  301.8 0.2 fusion.8
  302.0 0.1 copy.102
  302.2 0.1 multiply_convert_fusion
  302.3 6.1 %collective-permute-start.4 = (bf16[16,1,512]{2,1,0:T(2,128)(2,1)S(1)}, bf16[16,1,512]{2,1,0:T(2,128)(2,1)S(1)}, u32[]{:S(2)}, u32[]{:S(2)}) collective-permute-start(bf16[16,1,512]{2,1,0:T(2,128)(2,1)S(1)} %get-tuple-element.12), channel_id=1, source_target_pairs={{0,8},{8,16},{16,24},{24,32},{32,40},{40,48},{48,56},{56,64},{64,7... | collective-permute-start | bytes 49160 | tf_op jit(solution)/shard_map/ppermute | solution.py:21
  308.5 1.9 collective-permute-start.5
  310.4 12.0 %collective-permute-done.5 = bf16[16,1,512]{2,1,0:T(2,128)(2,1)S(1)} collective-permute-done((bf16[16,1,512]{2,1,0:T(2,128)(2,1)S(1)}, bf16[16,1,512]{2,1,0:T(2,128)(2,1)S(1)}, u32[]{:S(2)}, u32[]{:S(2)}) %collective-permute-start.5) | collective-permute-done | bytes 16416 | tf_op jit(solution)/shard_map/ppermute | solution.py:22
  322.4 1.9 collective-permute-start.6
  324.4 5.4 %collective-permute-start.7 = (bf16[1,6,512]{2,1,0:T(8,128)(2,1)S(1)}, bf16[1,6,512]{2,1,0:T(8,128)(2,1)S(1)}, u32[]{:S(2)}, u32[]{:S(2)}) collective-permute-start(bf16[1,6,512]{2,1,0:T(8,128)(2,1)S(1)} %get-tuple-element.9), channel_id=1, source_target_pairs={{1,0},{2,1},{3,2},{4,3},{5,4},{6,5},{7,6},{0,7},{9,8},{10,9},{11,1... | collective-permute-start | bytes 18440 | tf_op jit(solution)/shard_map/ppermute | solution.py:22
  329.8 1.3 collective-permute-done.7
  331.2 4.2 %fusion.20 = f32[18,6,9,512]{3,1,2,0:T(8,128)S(1)} fusion(bf16[9,512,512,1]{2,1,0,3:T(8,128)(2,1)} %bitcast.109, bf16[1,6,512]{2,1,0:T(8,128)(2,1)S(1)} %collective-permute-done.7, bf16[16,1,512]{2,1,0:T(2,128)(2,1)S(1)} %collective-permute-done.5, bf16[16,4,512]{2,1,0:T(4,128)(2,1)S(1)} %reshape.177, bf16[16,1,512]{2,1,0:T(2,128)(2,1)S(1)} %collective-permute-done.4, ...), kind=kOutput, calls=%fused_computation.38 | convolution fusion | flops 510271488 | bytes 6819876 | tf_op jit(solution)/shard_map/ec,nc->en/dot_general | solution.py:141
  335.3 0.9 fusion.37
  (41 shorter events, 0.9 us)
Async XLA Ops:
  6.5 13.7 %copy-start = (bf16[512,512]{1,0:T(8,128)(2,1)S(1)}, bf16[512,512]{1,0:T(8,128)(2,1)}, u32[]{:S(2)}) copy-start(bf16[512,512]{1,0:T(8,128)(2,1)} %param.10) | copy-start | bytes 1572868
  6.5 171.1 %all-gather.2.cloned.1.call-start = ((), (), s32[]{:S(2)}) async-start(), calls=%async_computation.7 | async-start | bytes 4792320 | tf_op jit(solution)/shard_map/all_gather | solution.py:94
  8.2 27.0 %collective-permute-start = (bf16[16,1,512]{2,1,0:T(2,128)(2,1)S(1)}, bf16[16,1,512]{2,1,0:T(2,128)(2,1)S(1)}, u32[]{:S(2)}, u32[]{:S(2)}) collective-permute-start(bf16[16,1,512]{2,1,0:T(2,128)(2,1)S(1)} %get-tuple-element.14), channel_id=1, source_target_pairs={{0,8},{8,16},{16,24},{24,32},{32,40},{40,48},{48,56},{56,64},{64,7... | collective-permute-start | bytes 49160 | tf_op jit(solution)/shard_map/ppermute | solution.py:21
  18.3 16.9 %collective-permute-start.1 = (bf16[16,1,512]{2,1,0:T(2,128)(2,1)S(1)}, bf16[16,1,512]{2,1,0:T(2,128)(2,1)S(1)}, u32[]{:S(2)}, u32[]{:S(2)}) collective-permute-start(bf16[16,1,512]{2,1,0:T(2,128)(2,1)S(1)} %get-tuple-element.15), channel_id=1, source_target_pairs={{8,0},{16,8},{24,16},{32,24},{40,32},{48,40},{56,48},{64,56},{72,6... | collective-permute-start | bytes 49160 | tf_op jit(solution)/shard_map/ppermute | solution.py:22
  22.1 160.2 %all-to-all-start.2 = ((bf16[64,1,4,128]{3,2,1,0:T(4,128)(2,1)}), bf16[64,1,4,128]{3,2,1,0:T(4,128)(2,1)S(1)}, u32[]{:S(2)}, u32[]{:S(2)}) async-start(bf16[64,1,4,128]{3,2,1,0:T(4,128)(2,1)} %copy.88), calls=%async_computation.2 | async-start | bytes 131072 | tf_op jit(solution)/shard_map/all_to_all | solution.py:122
  35.9 9.2 %collective-permute-start.2 = (bf16[1,6,512]{2,1,0:T(8,128)(2,1)S(1)}, bf16[1,6,512]{2,1,0:T(8,128)(2,1)S(1)}, u32[]{:S(2)}, u32[]{:S(2)}) collective-permute-start(bf16[1,6,512]{2,1,0:T(8,128)(2,1)S(1)} %get-tuple-element.10), channel_id=1, source_target_pairs={{0,1},{1,2},{2,3},{3,4},{4,5},{5,6},{6,7},{7,0},{8,9},{9,10},{10,1... | collective-permute-start | bytes 18440 | tf_op jit(solution)/shard_map/ppermute | solution.py:21
  37.9 7.3 %collective-permute-start.3 = (bf16[1,6,512]{2,1,0:T(8,128)(2,1)S(1)}, bf16[1,6,512]{2,1,0:T(8,128)(2,1)S(1)}, u32[]{:S(2)}, u32[]{:S(2)}) collective-permute-start(bf16[1,6,512]{2,1,0:T(8,128)(2,1)S(1)} %get-tuple-element.11), channel_id=1, source_target_pairs={{1,0},{2,1},{3,2},{4,3},{5,4},{6,5},{7,6},{0,7},{9,8},{10,9},{11,1... | collective-permute-start | bytes 18440 | tf_op jit(solution)/shard_map/ppermute | solution.py:22
  43.4 1.8 copy-start.1
  45.2 132.5 %copy-start.3 = (f32[512]{0:T(512)S(1)}, f32[512]{0:T(512)}, u32[]{:S(2)}) copy-start(f32[512]{0:T(512)} %param.8) | copy-start | bytes 6148
  182.3 19.3 %all-to-all-start.1 = ((bf16[64,1,4,128]{3,2,1,0:T(4,128)(2,1)}), bf16[64,1,4,128]{3,2,1,0:T(4,128)(2,1)S(1)}, u32[]{:S(2)}, u32[]{:S(2)}) async-start(bf16[64,1,4,128]{3,2,1,0:T(4,128)(2,1)} %copy.85), calls=%async_computation.1 | async-start | bytes 131072 | tf_op jit(solution)/shard_map/all_to_all | solution.py:116
  201.6 19.3 %all-to-all-start = ((bf16[64,1,4,128]{3,2,1,0:T(4,128)(2,1)}), bf16[64,1,4,128]{3,2,1,0:T(4,128)(2,1)S(1)}, u32[]{:S(2)}, u32[]{:S(2)}) async-start(bf16[64,1,4,128]{3,2,1,0:T(4,128)(2,1)} %copy.83), calls=%async_computation | async-start | bytes 131072 | tf_op jit(solution)/shard_map/all_to_all | solution.py:113
  220.9 19.3 %all-to-all-start.3 = ((bf16[64,1,4,128]{3,2,1,0:T(4,128)(2,1)}), bf16[64,1,4,128]{3,2,1,0:T(4,128)(2,1)S(1)}, u32[]{:S(2)}, u32[]{:S(2)}) async-start(bf16[64,1,4,128]{3,2,1,0:T(4,128)(2,1)} %copy.90), calls=%async_computation.3 | async-start | bytes 131072 | tf_op jit(solution)/shard_map/all_to_all | solution.py:119
  243.3 19.3 %all-to-all-start.4 = ((bf16[64,2,256]{2,1,0:T(2,128)(2,1)}), bf16[64,2,256]{2,1,0:T(2,128)(2,1)S(1)}, u32[]{:S(2)}, u32[]{:S(2)}) async-start(bf16[64,2,256]{2,1,0:T(2,128)(2,1)} %reshape.201), calls=%async_computation.4 | async-start | bytes 131072 | tf_op jit(solution)/shard_map/all_to_all | solution.py:58
  262.6 19.3 %all-to-all-start.5 = ((bf16[64,2,256]{2,1,0:T(2,128)(2,1)}), bf16[64,2,256]{2,1,0:T(2,128)(2,1)S(1)}, u32[]{:S(2)}, u32[]{:S(2)}) async-start(bf16[64,2,256]{2,1,0:T(2,128)(2,1)} %reshape.199), calls=%async_computation.5 | async-start | bytes 131072 | tf_op jit(solution)/shard_map/all_to_all | solution.py:59
  271.5 30.3 %copy-start.2 = (bf16[16,4,512]{2,1,0:T(4,128)(2,1)S(1)}, bf16[16,4,512]{2,1,0:T(4,128)(2,1)}, u32[]{:S(2)}) copy-start(bf16[16,4,512]{2,1,0:T(4,128)(2,1)} %param.11) | copy-start | bytes 196612
  281.8 19.5 %all-to-all-start.6 = ((bf16[64,2,256]{2,1,0:T(2,128)(2,1)}), bf16[64,2,256]{2,1,0:T(2,128)(2,1)S(1)}, u32[]{:S(2)}, u32[]{:S(2)}) async-start(bf16[64,2,256]{2,1,0:T(2,128)(2,1)} %reshape.197), calls=%async_computation.6 | async-start | bytes 131072 | tf_op jit(solution)/shard_map/all_to_all | solution.py:60
  302.3 8.1 %collective-permute-start.4 = (bf16[16,1,512]{2,1,0:T(2,128)(2,1)S(1)}, bf16[16,1,512]{2,1,0:T(2,128)(2,1)S(1)}, u32[]{:S(2)}, u32[]{:S(2)}) collective-permute-start(bf16[16,1,512]{2,1,0:T(2,128)(2,1)S(1)} %get-tuple-element.12), channel_id=1, source_target_pairs={{0,8},{8,16},{16,24},{24,32},{32,40},{40,48},{48,56},{56,64},{64,7... | collective-permute-start | bytes 49160 | tf_op jit(solution)/shard_map/ppermute | solution.py:21
  308.5 13.9 %collective-permute-start.5 = (bf16[16,1,512]{2,1,0:T(2,128)(2,1)S(1)}, bf16[16,1,512]{2,1,0:T(2,128)(2,1)S(1)}, u32[]{:S(2)}, u32[]{:S(2)}) collective-permute-start(bf16[16,1,512]{2,1,0:T(2,128)(2,1)S(1)} %get-tuple-element.13), channel_id=1, source_target_pairs={{8,0},{16,8},{24,16},{32,24},{40,32},{48,40},{56,48},{64,56},{72,6... | collective-permute-start | bytes 49160 | tf_op jit(solution)/shard_map/ppermute | solution.py:22
  322.4 7.4 %collective-permute-start.6 = (bf16[1,6,512]{2,1,0:T(8,128)(2,1)S(1)}, bf16[1,6,512]{2,1,0:T(8,128)(2,1)S(1)}, u32[]{:S(2)}, u32[]{:S(2)}) collective-permute-start(bf16[1,6,512]{2,1,0:T(8,128)(2,1)S(1)} %get-tuple-element.8), channel_id=1, source_target_pairs={{0,1},{1,2},{2,3},{3,4},{4,5},{5,6},{6,7},{7,0},{8,9},{9,10},{10,1... | collective-permute-start | bytes 18440 | tf_op jit(solution)/shard_map/ppermute | solution.py:21
  324.4 6.8 %collective-permute-start.7 = (bf16[1,6,512]{2,1,0:T(8,128)(2,1)S(1)}, bf16[1,6,512]{2,1,0:T(8,128)(2,1)S(1)}, u32[]{:S(2)}, u32[]{:S(2)}) collective-permute-start(bf16[1,6,512]{2,1,0:T(8,128)(2,1)S(1)} %get-tuple-element.9), channel_id=1, source_target_pairs={{1,0},{2,1},{3,2},{4,3},{5,4},{6,5},{7,6},{0,7},{9,8},{10,9},{11,1... | collective-permute-start | bytes 18440 | tf_op jit(solution)/shard_map/ppermute | solution.py:22
Sparse Core Ops, SparseCore 0:
  11.8 165.7 all-gather.1
where the time goes:
time: 344 us; the launch traced here: 343 us
  waiting for transfers between devices  203 us (59%)
  starting transfers between devices  100 us (29%)
  between operations  13.9 us (4%)
  matrix products  11 us (3%)
  local copies, waits for them, and re-layouts  9.54 us (3%)
  other arithmetic  5.13 us (1%)
    all_gather x1, waiting for transfers between devices, body(): lax.all_gather(conv_weight, 'lon', axis=0, tiled=True)  132 us
    ppermute x4, starting transfers between devices, extended_2(): before = lax.ppermute(last, axis, up)  20 us
    ppermute x4, starting transfers between devices, extended_2(): after = lax.ppermute(initial, axis, down)  14.7 us
    ppermute x4, waiting for transfers between devices, extended_2(): after = lax.ppermute(initial, axis, down)  13.3 us
    all_to_all x1, starting transfers between devices, body(): lax.all_to_all(out_grad.reshape(layout), 'lon', split_axis=0, concat_axis...  13.1 us
    all_to_all x1, waiting for transfers between devices, attend_rows(): lax.all_to_all(grad_value, 'lon', split_axis=2, concat_axis=0, tiled=True)  10.4 us
    all_to_all x1, waiting for transfers between devices, body(): lax.all_to_all(projected[2].reshape(layout), 'lon', split_axis=0, concat_...  10.3 us
    all_to_all x1, waiting for transfers between devices, body(): lax.all_to_all(projected[1].reshape(layout), 'lon', split_axis=0, concat_...  9.88 us
  transfers between devices with their start and end apart: 16, of which 9 were waited for; matrix products, arithmetic and copies ran while one was open for 5% of the time, Pallas kernels for 0%

commit v1 on v0

v1 whole, which is shorter than its diff:
```python
import functools
import math

import jax
import jax.numpy as jnp
from jax import lax
from jax.experimental import pallas as pl
from jax.experimental.pallas import tpu as pltpu
from jax.sharding import PartitionSpec as P

X = 4
Y = 8
ZY = 16
LATS = 8
ROWS = ZY * LATS
CAP = 20.0
INV_ROOT = 1.0 / math.sqrt(128.0)
F32 = jnp.float32
BF16 = jnp.bfloat16
VMEM_LIMIT = 60 * 1024 * 1024

NN = (((1,), (0,)), ((), ()))
NT = (((1,), (1,)), ((), ()))
TN = (((0,), (0,)), ((), ()))


def dot(a, b, dims=NN):
    return lax.dot_general(a, b, dims, preferred_element_type=F32)


def kernel(
    st_hbm, ct_hbm, cw_hbm, bias_hbm, wqkv, wout, out,
    raw, raw_w, st, ct, wp, bias,
    rows, cots, flat, grid, cot_grid, cot_blocks, w_one, w_all, wq, wo,
    pre, acts, blocks, parts, parts_in, own_pre, pres, shifted, mine, sums_in, rims, rims_in,
    load_sem, w_send, w_recv, row_send, row_recv, cot_send, cot_recv, pre_send, pre_recv,
    end_send, rim_send, rim_recv,
    send, recv,
):
    lon = lax.axis_index("lon")
    lat = lax.axis_index("lat")
    zy, x = lon // X, lon % X
    z, y = zy // Y, zy % Y
    core = lat % 2
    sib = lat + 1 - 2 * core
    row = lat * ZY + zy
    up, down = (lat + 1) % LATS, (lat + LATS - 1) % LATS
    after, before = (row + 1) % ROWS, (row + ROWS - 1) % ROWS
    east, west = (x + 1) % X, (x + X - 1) % X

    def remote(src, dst, send_sem, recv_sem, to_zy, to_x, to_lat):
        return pltpu.make_async_remote_copy(
            src_ref=src,
            dst_ref=dst,
            send_sem=send_sem,
            recv_sem=recv_sem,
            device_id={"lon": to_zy * X + to_x, "lat": to_lat},
            device_id_type=pl.DeviceIdType.MESH,
        )

    started = []

    def push_to(src, dst, to_zy, to_x, to_lat):
        i = len(started)
        copy = remote(src, dst, send.at[i], recv.at[i], to_zy, to_x, to_lat)
        copy.start()
        started.append(copy)
        return copy

    def push(ref, to_zy, to_x, to_lat):
        return push_to(ref, ref, to_zy, to_x, to_lat)

    def load(i, src, dst):
        copy = pltpu.make_async_copy(src, dst, load_sem.at[i])
        copy.start()
        return copy

    weight_load = load(0, cw_hbm, raw_w)
    state_load = load(1, st_hbm, raw.at[0])
    cot_load = load(2, ct_hbm, raw.at[1])
    loads = [load(3, bias_hbm, bias)]
    for t in range(3):
        source = wqkv.at[:, pl.ds(pl.multiple_of(t * 512 + x * 128, 128), 128)]
        loads.append(load(4 + t, source, wq.at[:, 128 * t : 128 * (t + 1)]))
    loads.append(load(7, wout.at[pl.ds(pl.multiple_of(x * 128, 128), 128)], wo))

    barrier = pltpu.get_barrier_semaphore()

    def hello(to_zy, to_x, to_lat):
        pl.semaphore_signal(
            barrier,
            inc=1,
            device_id={"lon": to_zy * X + to_x, "lat": to_lat},
            device_id_type=pl.DeviceIdType.MESH,
        )

    other_zy = (1 - z) * Y + y
    for dx in range(1, X):
        hello(zy, (x + dx) % X, lat)
        hello(other_zy, (x + dx) % X, lat)
    hello(zy, x, sib)

    @pl.loop(1, ZY)
    def _(d):
        hello((zy + d) % ZY, x, lat)

    hello(ZY - 1, x, down)
    hello(0, x, up)

    @pl.when(x == 0)
    def _():
        for i in range(X):
            hello((zy + ZY - 1) % ZY, i, lat)

    @pl.when(x == X - 1)
    def _():
        for i in range(X):
            hello((zy + 1) % ZY, i, lat)

    weight_load.wait()
    for q in range(X):
        piece = raw_w[:, 128 * q : 128 * (q + 1)].astype(F32)
        wp[q] = jnp.concatenate([piece, jnp.zeros((8, 128), F32)], axis=0).astype(BF16)

    edge = (zy == 0) | (zy == ZY - 1)
    pl.semaphore_wait(barrier, 2 * (X - 1) + (ZY - 1) + 1 + 2 + jnp.where(edge, ZY, 0))

    def all_weights(start):
        @pl.when(x // 2 == core)
        def _():
            slot = z * 2 + x % 2
            for t in range(2 * X):
                to_z, to_x = t // X, t % X
                here = (to_z == z) & (to_x == x)
                if start:
                    @pl.when(here)
                    def _():
                        pltpu.make_async_copy(
                            wp.at[to_x], w_one.at[slot], w_recv.at[slot]
                        ).start()

                @pl.when(jnp.logical_not(here))
                def _():
                    copy = remote(
                        wp.at[to_x], w_one.at[slot], w_send.at[t], w_recv.at[slot],
                        to_z * Y + y, to_x, lat,
                    )
                    if start:
                        copy.start()
                    else:
                        copy.wait_send()

    all_weights(True)

    def relayout(which, dst):
        for r in range(16):
            for q in range(4):
                piece = raw[which, r, :, 128 * q : 128 * (q + 1)].astype(F32)
                flat[pl.ds(16 * r + q, 4, stride=4), :] = piece
        dst[...] = flat[0:256, :].astype(BF16).reshape(16, 16, 128)

    state_load.wait()
    relayout(0, st)

    def all_rows(src, dst, send_sem, recv_sem, start, first=0, last=ZY):
        @pl.loop(first, last)
        def _(t):
            if start:
                @pl.when(t == zy)
                def _():
                    pltpu.make_async_copy(src.at[t], dst, recv_sem).start()

            @pl.when(t != zy)
            def _():
                copy = remote(src.at[t], dst, send_sem.at[t], recv_sem, t, x, lat)
                if start:
                    copy.start()
                else:
                    copy.wait_send()

    all_rows(st, rows.at[1, zy, x], row_send, row_recv, True)

    for i in range(4):
        pltpu.make_async_copy(w_one.at[i], w_one.at[i], w_recv.at[i]).wait()

    def half(place, which):
        return pl.ds(pl.multiple_of((place * 2 + which) * 144, 16), 144)

    for i in range(2):
        both = [w_one[2 * i + s].astype(F32)[:72] for s in range(2)]
        w_all[i, half(y, core), :] = jnp.concatenate(both, axis=0).astype(BF16)

    right = z * Y + (y + 1) % Y
    left = z * Y + (y + Y - 1) % Y

    def ring(part, place, to):
        return push(w_all.at[part, half(place, core)], to, x, lat)

    rights = [[ring(0, y, right), ring(1, y, right)]]
    lefts = [[ring(1, y, left), ring(0, y, left)]]
    pair = [push(w_all.at[:, half(y, core)], zy, x, sib)]

    def forward(step):
        turns = (
            (rights, right, (y + Y - 1 - step) % Y, (0, 1)),
            (lefts, left, (y + 1 + step) % Y, (1, 0)),
        )
        for copies, _, _, _ in turns:
            copies.append([])
        for turn in range(len(rights[step])):
            for copies, to, got, parts_of in turns:
                copies[step][turn].wait_recv()
                part = parts_of[turn]
                if step < 2 or (step == 2 and turn == 0):
                    copies[step + 1].append(ring(part, got, to))
                pair.append(push(w_all.at[part, half(got, core)], zy, x, sib))

    pltpu.make_async_copy(rows.at[1, :, x], rows.at[1, :, x], row_recv).wait()
    to_after = push_to(rows.at[1, :, x], rows.at[0, :, x], after % ZY, x, after // ZY)
    to_before = push_to(rows.at[1, :, x], rows.at[2, :, x], before % ZY, x, before // ZY)
    row_east = push(rows.at[1, :, x], zy, east, lat)
    row_west = push(rows.at[1, :, x], zy, west, lat)

    cot_load.wait()
    relayout(1, ct)
    forward(0)

    to_after.wait_recv()
    to_before.wait_recv()
    above_east = push(rows.at[0, :, x], zy, east, lat)
    below_west = push(rows.at[2, :, x], zy, west, lat)
    below_east = push(rows.at[2, :, x], zy, east, lat)
    above_west = push(rows.at[0, :, x], zy, west, lat)
    row_east.wait_recv()
    row_on_east = push(rows.at[1, 0:8, west], zy, east, lat)
    row_west.wait_recv()
    row_on_west = push(rows.at[1, 8:16, east], zy, west, lat)

    forward(1)

    all_rows(ct, cots.at[zy, x], cot_send, cot_recv, True)
    above_east.wait_recv()
    above_on = push(rows.at[0, :, west], zy, east, lat)
    below_west.wait_recv()
    below_on = push(rows.at[2, :, east], zy, west, lat)

    forward(2)

    def whole_row(a):
        flat[...] = rows[a].reshape(1024, 128).astype(F32)
        for q in range(4):
            part = flat[pl.ds(q, 256, stride=4), :]
            if a == 0:
                part = jnp.where(row == 0, 0.0, part)
            if a == 2:
                part = jnp.where(row == ROWS - 1, 0.0, part)
            grid[a, :, 128 * q : 128 * (q + 1)] = part.astype(BF16)

    row_on_east.wait_recv()
    row_on_west.wait_recv()
    whole_row(1)

    pltpu.make_async_copy(cots.at[:, x], cots.at[:, x], cot_recv).wait()
    cot_x = [push(cots.at[:, x], zy, (x + dx) % X, lat) for dx in range(1, X)]

    forward(3)

    below_east.wait_recv()
    above_west.wait_recv()
    above_on.wait_recv()
    whole_row(0)
    below_on.wait_recv()
    whole_row(2)
    for copy in loads:
        copy.wait()
    for copy in pair:
        copy.wait_recv()

    def tap(i):
        if i < 4:
            return w_all[0, 512 * i : 512 * (i + 1), :]
        if i > 4:
            return w_all[1, 512 * i - 2304 : 512 * (i + 1) - 2304, :]
        return jnp.concatenate([w_all[0, 2048:2304, :], w_all[1, 0:256, :]], axis=0)

    two = jnp.zeros((256, 256), F32)
    third = jnp.zeros((256, 128), F32)
    for a in (1, 0, 2):
        two = two + dot(grid[a], jnp.concatenate([tap(3 * a), tap(3 * a + 1)], axis=1))
        third = third + dot(grid[a], tap(3 * a + 2))
    preact = (
        bias[pl.ds(x, 1), :]
        + pltpu.roll(two[:, 0:128], 1, 0)
        + two[:, 128:256]
        + pltpu.roll(third, 255, 0)
    )
    pre[...] = preact
    acts[x] = (preact * jax.nn.sigmoid(preact)).astype(BF16)
    act_x = [push(acts.at[x], zy, (x + dx) % X, lat) for dx in range(1, X)]

    for copy in cot_x:
        copy.wait_recv()
    flat[...] = cots[...].reshape(1024, 128).astype(F32)
    for q in range(4):
        part = flat[pl.ds(q, 256, stride=4), :].astype(BF16)
        cot_grid[:, 128 * q : 128 * (q + 1)] = part
        cot_blocks[q] = part
    out_grad = dot(cot_grid[...], wo[...], NT).astype(BF16)

    for copy in act_x:
        copy.wait_recv()
    activated = jnp.concatenate([acts[s] for s in range(X)], axis=1)
    projected = dot(activated, wq[...]).astype(BF16)
    queries, keys, values = (projected[:, 128 * t : 128 * (t + 1)] for t in range(3))
    capped = jnp.tanh(dot(queries, keys, NT) * (INV_ROOT / CAP))
    expo = jnp.exp(CAP * capped)
    probs = expo / jnp.sum(expo, axis=-1, keepdims=True)
    probs_b = probs.astype(BF16)
    attended = dot(probs_b, values).astype(BF16)
    centre = jnp.sum(out_grad.astype(F32) * attended.astype(F32), axis=-1, keepdims=True)
    score_grad = (
        probs * (dot(out_grad, values, NT) - centre) * (1.0 - capped * capped) * INV_ROOT
    ).astype(BF16)
    grads = jnp.concatenate(
        [
            dot(score_grad, keys).astype(BF16),
            dot(score_grad, queries, TN).astype(BF16),
            dot(probs_b, out_grad, TN).astype(BF16),
        ],
        axis=1,
    )
    head_part = dot(grads, wq[...], NT)
    for q in range(X):
        blocks[q] = head_part[:, 128 * q : 128 * (q + 1)]

    part_x = []
    for half_of in range(2):
        at = slice(128 * half_of, 128 * (half_of + 1))
        for dx in (2, 1, 3):
            to = (x + dx) % X
            parts[dx - 1, at] = blocks[to, at].astype(BF16)
            part_x.append(
                push_to(parts.at[dx - 1, at], parts_in.at[dx - 1, at], zy, to, lat)
            )

    def all_pres(first, start):
        all_rows(own_pre, pres.at[1 + zy], pre_send, pre_recv, start, first, first + 8)

        def ends(slot, to_lat):
            @pl.loop(first, first + 8)
            def _(t):
                copy = remote(
                    own_pre.at[t], pres.at[slot], end_send.at[t], pre_recv, t, x, to_lat
                )
                if start:
                    copy.start()
                else:
                    copy.wait_send()

        @pl.when(zy == ZY - 1)
        def _():
            ends(0, up)

        @pl.when(zy == 0)
        def _():
            ends(ZY + 1, down)

    for half_of in range(2):
        at = slice(128 * half_of, 128 * (half_of + 1))
        grad_act = blocks[x, at] + cot_blocks[x, at].astype(F32)
        preact = pre[at]
        s = jax.nn.sigmoid(preact)
        slope = s * (1.0 + preact * (1.0 - s))
        for copy in part_x[3 * half_of : 3 * half_of + 3]:
            copy.wait_recv()
        for i in range(X - 1):
            grad_act = grad_act + parts_in[i, at].astype(F32)
        own_pre[8 * half_of : 8 * (half_of + 1)] = (
            (grad_act * slope).astype(BF16).reshape(8, 16, 128)
        )
        all_pres(8 * half_of, True)

    pltpu.make_async_copy(pres, pres, pre_recv).wait()

    @pl.when(lat == 0)
    def _():
        pres[0] = jnp.zeros((16, 128), BF16)

    @pl.when(lat == LATS - 1)
    def _():
        pres[ZY + 1] = jnp.zeros((16, 128), BF16)

    around = jnp.concatenate(
        [pres[2 - a : 2 - a + ZY].reshape(256, 128) for a in range(3)], axis=1
    )
    column = lax.broadcasted_iota(jnp.int32, (256, 256), 0) % 16
    sum_x = []
    for h in range(2):
        at = slice(256 * h, 256 * (h + 1))
        result = jnp.zeros((256, 256), F32)
        for b in range(3):
            taps = jnp.concatenate([tap(3 * a + b)[at] for a in range(3)], axis=1)
            acc = dot(around, taps, NT)
            if b != 1:
                for q in range(2):
                    shifted[...] = acc[:, 128 * q : 128 * (q + 1)]
                    rim = shifted[pl.ds(0 if b == 0 else 15, 16, stride=16), :]
                    rims[b // 2, h, q] = rim.astype(BF16)
            if b == 0:
                acc = jnp.where(column == 15, 0.0, pltpu.roll(acc, 255, 0))
            if b == 2:
                acc = jnp.where(column == 0, 0.0, pltpu.roll(acc, 1, 0))
            result = result + acc
        for q in range(2):
            base = 512 * h + 256 * q
            flat[base : base + 256, :] = result[:, 128 * q : 128 * (q + 1)]
            for to in range(X):
                for j in range(4):
                    piece = flat[pl.ds(base + 4 * to + j, 16, stride=16), :]
                    mine[to, h, q, j] = piece.astype(BF16)
        for dx in (2, 1, 3):
            to = (x + dx) % X
            sum_x.append(push_to(mine.at[to, h], sums_in.at[dx - 1, h], zy, to, lat))

    rim_west = remote(
        rims.at[0], rims_in.at[x], rim_send.at[0], rim_recv.at[x],
        (zy + ZY - 1) % ZY, X - 1, lat,
    )
    rim_east = remote(
        rims.at[1], rims_in.at[x], rim_send.at[1], rim_recv.at[x], (zy + 1) % ZY, 0, lat
    )
    rim_west.start()
    rim_east.start()

    for h in range(2):
        total = mine[x, h].astype(F32)
        for copy in sum_x[3 * h : 3 * h + 3]:
            copy.wait_recv()
        for i in range(X - 1):
            total = total + sums_in[i, h].astype(F32)
        flat[128 * h : 128 * (h + 1), :] = total.reshape(128, 128)

    def add_rims(j):
        for i in range(X):
            pltpu.make_async_copy(rims_in.at[i], rims_in.at[i], rim_recv.at[i]).wait()
        for q in range(4):
            at = slice(64 * q + 16 * j, 64 * q + 16 * (j + 1))
            total = flat[at]
            for i in range(X):
                total = total + rims_in[i, q // 2, q % 2].astype(F32)
            flat[at] = total

    @pl.when(x == 0)
    def _():
        add_rims(0)

    @pl.when(x == X - 1)
    def _():
        add_rims(3)

    for t in range(ZY):
        out[t] = flat[pl.ds(t, 16, stride=16), :].astype(BF16)

    rim_west.wait_send()
    rim_east.wait_send()
    for copy in started:
        copy.wait_send()
    all_weights(False)
    all_rows(st, rows.at[1, zy, x], row_send, row_recv, False)
    all_rows(ct, cots.at[zy, x], cot_send, cot_recv, False)
    all_pres(0, False)
    all_pres(8, False)


PUSHES = 64


def body(state, conv_weight, conv_bias, w_qkv, w_out, cotangent):
    vmem = pl.BlockSpec(memory_space=pltpu.VMEM)
    anywhere = pl.BlockSpec(memory_space=pl.ANY)
    dma = pltpu.SemaphoreType.DMA
    out = pl.pallas_call(
        kernel,
        out_shape=jax.ShapeDtypeStruct((ZY, 16, 128), BF16),
        in_specs=[anywhere] * 6,
        out_specs=vmem,
        scratch_shapes=[
            pltpu.VMEM((2, 16, 4, 512), BF16),
            pltpu.VMEM((72, 512), BF16),
            pltpu.VMEM((ZY, 16, 128), BF16),
            pltpu.VMEM((ZY, 16, 128), BF16),
            pltpu.VMEM((X, 80, 128), BF16),
            pltpu.VMEM((X, 128), F32),
            pltpu.VMEM((3, ZY, X, 16, 128), BF16),
            pltpu.VMEM((ZY, X, 16, 128), BF16),
            pltpu.VMEM((1024, 128), F32),
            pltpu.VMEM((3, 256, 512), BF16),
            pltpu.VMEM((256, 512), BF16),
            pltpu.VMEM((4, 256, 128), BF16),
            pltpu.VMEM((4, 80, 128), BF16),
            pltpu.VMEM((2, 2304, 128), BF16),
            pltpu.VMEM((512, 384), BF16),
            pltpu.VMEM((128, 512), BF16),
            pltpu.VMEM((256, 128), F32),
            pltpu.VMEM((X, 256, 128), BF16),
            pltpu.VMEM((X, 256, 128), F32),
            pltpu.VMEM((3, 256, 128), BF16),
            pltpu.VMEM((3, 256, 128), BF16),
            pltpu.VMEM((ZY, 16, 128), BF16),
            pltpu.VMEM((ZY + 2, 16, 128), BF16),
            pltpu.VMEM((256, 128), F32),
            pltpu.VMEM((X, 2, 2, 4, ZY, 128), BF16),
            pltpu.VMEM((3, 2, 2, 4, ZY, 128), BF16),
            pltpu.VMEM((2, 2, 2, ZY, 128), BF16),
            pltpu.VMEM((X, 2, 2, ZY, 128), BF16),
            dma((8,)),
            dma((2 * X,)),
            dma((4,)),
            dma((ZY,)),
            dma,
            dma((ZY,)),
            dma,
            dma((ZY,)),
            dma,
            dma((ZY,)),
            dma((2,)),
            dma((X,)),
            dma((PUSHES,)),
            dma((PUSHES,)),
        ],
        compiler_params=pltpu.CompilerParams(
            collective_id=0, has_side_effects=True, vmem_limit_bytes=VMEM_LIMIT
        ),
    )(state, cotangent, conv_weight, conv_bias.reshape(X, 128), w_qkv, w_out)
    return out.reshape(16, 4, 4, 128).transpose(0, 2, 1, 3).reshape(16, 4, 512)


def solution(mesh):
    return jax.shard_map(
        body,
        mesh=mesh,
        in_specs=(P("lat", "lon", None), P("lon", None), P(), P(), P(), P("lat", "lon", None)),
        out_specs=P("lat", "lon", None),
        check_vma=False,
    )
```

time: 344 us -> 71.9 us (0.21)
  the two profiles are of different devices: /device:TPU:62 before, /device:TPU:64 now
where the time goes in v1:
time: 71.9 us; the launch traced here: 71.7 us
  Pallas kernels  70.2 us (98%)
  local copies, waits for them, and re-layouts  1.49 us (2%)
    pallas_call x1, Pallas kernels, body(): pl.pallas_call(kernel, out_shape=jax.ShapeDtypeStruct((ZY, 16, 128), BF16...  70.2 us
    unnamed x1, local copies, waits for them, and re-layouts  1.49 us

profile of v1, /device:TPU:64, one launch (start us, length us, event | category | flops | bytes accessed | tf_op | source)
XLA Modules:
  0.0 71.7 jit_solution(12263343809008861893)
XLA Ops:
  0.0 70.2 %shard_map.64 = bf16[16,16,128]{2,1,0:T(8,128)(2,1)} custom-call(bf16[16,4,512]{2,1,0:T(4,128)(2,1)} %st_hbm.1, bf16[16,4,512]{2,1,0:T(4,128)(2,1)} %ct_hbm.1, bf16[72,512]{1,0:T(8,128)(2,1)} %cw_hbm.1, f32[4,128]{1,0:T(4,128)} %bitcast.7, bf16[512,1536]{1,0:T(8,128)(2,1)} %wqkv.1, bf16[512,512]{1,0:T(8,128)(2,1)} %wout.1), custom_call_target="tpu_custom_call" | custom-call | tf_op jit(solution)/shard_map/pallas_call | solution.py:482
  70.2 1.5 %copy.9 = bf16[16,4,512]{2,1,0:T(4,128)(2,1)} copy(bf16[16,4,512]{2,1,0:T(4,128)(2,1)} %bitcast.6) | data formatting | bytes 131072

commit v2 on v1

--- a/solution.py
+++ b/solution.py
@@ -34,7 +34,7 @@
     rows, cots, flat, grid, cot_grid, cot_blocks, w_one, w_all, wq, wo,
     pre, acts, blocks, parts, parts_in, own_pre, pres, shifted, mine, sums_in, rims, rims_in,
     load_sem, w_send, w_recv, row_send, row_recv, cot_send, cot_recv, pre_send, pre_recv,
-    end_send, rim_send, rim_recv,
+    end_send, rim_send, rim_recv, middle_send, side_send, side_recv,
     send, recv,
 ):
     lon = lax.axis_index("lon")
@@ -43,9 +43,13 @@
     z, y = zy // Y, zy % Y
     core = lat % 2
     sib = lat + 1 - 2 * core
-    row = lat * ZY + zy
+    mine_of = jnp.where(z == core, y, ZY - 1 - y)
+    row = lat * ZY + mine_of
     up, down = (lat + 1) % LATS, (lat + LATS - 1) % LATS
-    after, before = (row + 1) % ROWS, (row + ROWS - 1) % ROWS
+
+    def owner(t):
+        return jnp.where(t < Y, core * Y + t, (1 - core) * Y + ZY - 1 - t)
+
     east, west = (x + 1) % X, (x + X - 1) % X
 
     def remote(src, dst, send_sem, recv_sem, to_zy, to_x, to_lat):
@@ -97,15 +101,19 @@
     other_zy = (1 - z) * Y + y
     for dx in range(1, X):
         hello(zy, (x + dx) % X, lat)
-        hello(other_zy, (x + dx) % X, lat)
     hello(zy, x, sib)
 
     @pl.loop(1, ZY)
     def _(d):
         hello((zy + d) % ZY, x, lat)
 
-    hello(ZY - 1, x, down)
-    hello(0, x, up)
+    hello(core * Y, x, down)
+    hello((1 - core) * Y, x, up)
+
+    plane = lat // 2
+    near = jnp.where(plane < 2, 3, 0) * 2 + core
+    for i in range(2):
+        hello(other_zy, 2 * core + i, near)
 
     @pl.when(x == 0)
     def _():
@@ -122,33 +130,53 @@
         piece = raw_w[:, 128 * q : 128 * (q + 1)].astype(F32)
         wp[q] = jnp.concatenate([piece, jnp.zeros((8, 128), F32)], axis=0).astype(BF16)
 
-    edge = (zy == 0) | (zy == ZY - 1)
-    pl.semaphore_wait(barrier, 2 * (X - 1) + (ZY - 1) + 1 + 2 + jnp.where(edge, ZY, 0))
+    edge = (mine_of == 0) | (mine_of == ZY - 1)
+    sends_weight = x // 2 == core
+    crosses = sends_weight & ((plane == 0) | (plane == 3))
+    pl.semaphore_wait(
+        barrier,
+        (X - 1) + (ZY - 1) + 1 + 2 + jnp.where(edge, ZY, 0) + jnp.where(crosses, 2 * X, 0),
+    )
+
+    slot = z * 2 + x % 2
 
     def all_weights(start):
-        @pl.when(x // 2 == core)
+        def across(copy):
+            if start:
+                copy.start()
+            else:
+                copy.wait_send()
+
+        @pl.when(crosses)
         def _():
-            slot = z * 2 + x % 2
-            for t in range(2 * X):
-                to_z, to_x = t // X, t % X
-                here = (to_z == z) & (to_x == x)
+            for k in range(2):
+                to_lat = jnp.where(plane == 3, k, 2 + k) * 2 + core
+                for t in range(X):
+                    across(
+                        remote(
+                            wp.at[t], w_one.at[slot], w_send.at[X + X * k + t],
+                            w_recv.at[slot], other_zy, t, to_lat,
+                        )
+                    )
+
+        @pl.when(sends_weight)
+        def _():
+            for t in range(X):
                 if start:
-                    @pl.when(here)
+                    @pl.when(t == x)
                     def _():
                         pltpu.make_async_copy(
-                            wp.at[to_x], w_one.at[slot], w_recv.at[slot]
+                            wp.at[t], w_one.at[slot], w_recv.at[slot]
                         ).start()
 
-                @pl.when(jnp.logical_not(here))
+                @pl.when(t != x)
                 def _():
-                    copy = remote(
-                        wp.at[to_x], w_one.at[slot], w_send.at[t], w_recv.at[slot],
-                        to_z * Y + y, to_x, lat,
+                    across(
+                        remote(
+                            wp.at[t], w_one.at[slot], w_send.at[t], w_recv.at[slot],
+                            zy, t, lat,
+                        )
                     )
-                    if start:
-                        copy.start()
-                    else:
-                        copy.wait_send()
 
     all_weights(True)
 
@@ -162,89 +190,142 @@
     state_load.wait()
     relayout(0, st)
 
-    def all_rows(src, dst, send_sem, recv_sem, start, first=0, last=ZY):
-        @pl.loop(first, last)
+    def all_rows(src, dst, send_sem, recv_sem, start):
+        @pl.loop(0, ZY)
         def _(t):
             if start:
-                @pl.when(t == zy)
+                @pl.when(t == mine_of)
                 def _():
                     pltpu.make_async_copy(src.at[t], dst, recv_sem).start()
 
-            @pl.when(t != zy)
+            @pl.when(t != mine_of)
             def _():
-                copy = remote(src.at[t], dst, send_sem.at[t], recv_sem, t, x, lat)
+                copy = remote(
+                    src.at[t], dst, send_sem.at[t], recv_sem, owner(t), x, lat
+                )
                 if start:
                     copy.start()
                 else:
                     copy.wait_send()
 
+    def middle_rows(start):
+        for i, t, to in ((0, Y - 1, Y), (1, Y, Y - 1)):
+            dst = rows.at[2 * i, zy, x]
+            if start:
+                @pl.when(to == mine_of)
+                def _():
+                    pltpu.make_async_copy(st.at[t], dst, side_recv.at[i]).start()
+
+            @pl.when(to != mine_of)
+            def _():
+                copy = remote(
+                    st.at[t], dst, middle_send.at[i], side_recv.at[i], owner(to), x, lat
+                )
+                if start:
+                    copy.start()
+                else:
+                    copy.wait_send()
+
+    def side_rows(start):
+        for i, last, middle, to_lat, step in (
+            (0, ZY - 1, Y - 1, up, 1),
+            (1, 0, Y, down, -1),
+        ):
+            @pl.when(mine_of != middle)
+            def _():
+                to_zy = jnp.where(mine_of == last, zy, owner(mine_of + step))
+                copy = remote(
+                    rows.at[1, :, x], rows.at[2 * i, :, x], side_send.at[i], side_recv.at[i],
+                    to_zy, x, jnp.where(mine_of == last, to_lat, lat),
+                )
+                if start:
+                    copy.start()
+                else:
+                    copy.wait_send()
+
     all_rows(st, rows.at[1, zy, x], row_send, row_recv, True)
-
-    for i in range(4):
-        pltpu.make_async_copy(w_one.at[i], w_one.at[i], w_recv.at[i]).wait()
+    middle_rows(True)
 
     def half(place, which):
         return pl.ds(pl.multiple_of((place * 2 + which) * 144, 16), 144)
 
-    for i in range(2):
-        both = [w_one[2 * i + s].astype(F32)[:72] for s in range(2)]
-        w_all[i, half(y, core), :] = jnp.concatenate(both, axis=0).astype(BF16)
+    def take_weight(part):
+        both = []
+        for i in range(2):
+            at = w_one.at[2 * part + i]
+            pltpu.make_async_copy(at, at, w_recv.at[2 * part + i]).wait()
+            both.append(w_one[2 * part + i].astype(F32)[:72])
+        w_all[part, half(y, core), :] = jnp.concatenate(both, axis=0).astype(BF16)
 
     right = z * Y + (y + 1) % Y
     left = z * Y + (y + Y - 1) % Y
 
-    def ring(part, place, to):
-        return push(w_all.at[part, half(place, core)], to, x, lat)
-
-    rights = [[ring(0, y, right), ring(1, y, right)]]
-    lefts = [[ring(1, y, left), ring(0, y, left)]]
-    pair = [push(w_all.at[:, half(y, core)], zy, x, sib)]
-
-    def forward(step):
+    def ring(turn, place, to):
+        return push(w_all.at[(z, 1 - z)[turn], half(place, core)], to, x, lat)
+
+    rights = [[]]
+    lefts = [[]]
+    pair = []
+    for turn in range(2):
+        take_weight((z, 1 - z)[turn])
+        rights[0].append(ring(turn, y, right))
+        lefts[0].append(ring(turn, y, left))
+        pair.append(push(w_all.at[(z, 1 - z)[turn], half(y, core)], zy, x, sib))
+
+    def forward(step, turn):
         turns = (
-            (rights, right, (y + Y - 1 - step) % Y, (0, 1)),
-            (lefts, left, (y + 1 + step) % Y, (1, 0)),
+            (rights, right, (y + Y - 1 - step) % Y, 0),
+            (lefts, left, (y + 1 + step) % Y, 1),
         )
-        for copies, _, _, _ in turns:
-            copies.append([])
-        for turn in range(len(rights[step])):
-            for copies, to, got, parts_of in turns:
-                copies[step][turn].wait_recv()
-                part = parts_of[turn]
-                if step < 2 or (step == 2 and turn == 0):
-                    copies[step + 1].append(ring(part, got, to))
-                pair.append(push(w_all.at[part, half(got, core)], zy, x, sib))
-
+        for copies, to, got, last in turns:
+            if turn == 0:
+                copies.append([None, None])
+            copy = copies[step][turn]
+            if copy is None:
+                continue
+            copy.wait_recv()
+            if step < 2 or (step == 2 and turn == last):
+                copies[step + 1][turn] = ring(turn, got, to)
+            pair.append(push(w_all.at[(z, 1 - z)[turn], half(got, core)], zy, x, sib))
+
+    def round_x(whole, west_half, east_half):
+        return (
+            push(whole, zy, east, lat),
+            push(whole, zy, west, lat),
+            west_half,
+            east_half,
+        )
+
+    def round_x_on(to_east, to_west, west_half, east_half):
+        to_east.wait_recv()
+        on_east = push(west_half, zy, east, lat)
+        to_west.wait_recv()
+        return on_east, push(east_half, zy, west, lat)
+
+    forward(0, 0)
     pltpu.make_async_copy(rows.at[1, :, x], rows.at[1, :, x], row_recv).wait()
-    to_after = push_to(rows.at[1, :, x], rows.at[0, :, x], after % ZY, x, after // ZY)
-    to_before = push_to(rows.at[1, :, x], rows.at[2, :, x], before % ZY, x, before // ZY)
-    row_east = push(rows.at[1, :, x], zy, east, lat)
-    row_west = push(rows.at[1, :, x], zy, west, lat)
-
+    side_rows(True)
+    row_x = round_x(rows.at[1, :, x], rows.at[1, 0:8, west], rows.at[1, 8:16, east])
+    forward(0, 1)
     cot_load.wait()
     relayout(1, ct)
-    forward(0)
-
-    to_after.wait_recv()
-    to_before.wait_recv()
+    forward(1, 0)
+    row_on = round_x_on(*row_x)
+    for i in range(2):
+        at = rows.at[2 * i, :, x]
+        pltpu.make_async_copy(at, at, side_recv.at[i]).wait()
     above_east = push(rows.at[0, :, x], zy, east, lat)
     below_west = push(rows.at[2, :, x], zy, west, lat)
     below_east = push(rows.at[2, :, x], zy, east, lat)
     above_west = push(rows.at[0, :, x], zy, west, lat)
-    row_east.wait_recv()
-    row_on_east = push(rows.at[1, 0:8, west], zy, east, lat)
-    row_west.wait_recv()
-    row_on_west = push(rows.at[1, 8:16, east], zy, west, lat)
-
-    forward(1)
-
+    forward(1, 1)
+    forward(2, 0)
     all_rows(ct, cots.at[zy, x], cot_send, cot_recv, True)
     above_east.wait_recv()
     above_on = push(rows.at[0, :, west], zy, east, lat)
     below_west.wait_recv()
     below_on = push(rows.at[2, :, east], zy, west, lat)
-
-    forward(2)
+    forward(2, 1)
 
     def whole_row(a):
         flat[...] = rows[a].reshape(1024, 128).astype(F32)
@@ -256,14 +337,14 @@
                 part = jnp.where(row == ROWS - 1, 0.0, part)
             grid[a, :, 128 * q : 128 * (q + 1)] = part.astype(BF16)
 
-    row_on_east.wait_recv()
-    row_on_west.wait_recv()
+    for copy in row_on:
+        copy.wait_recv()
     whole_row(1)
+    forward(3, 0)
+    forward(3, 1)
 
     pltpu.make_async_copy(cots.at[:, x], cots.at[:, x], cot_recv).wait()
     cot_x = [push(cots.at[:, x], zy, (x + dx) % X, lat) for dx in range(1, X)]
-
-    forward(3)
 
     below_east.wait_recv()
     above_west.wait_recv()
@@ -296,7 +377,8 @@
     )
     pre[...] = preact
     acts[x] = (preact * jax.nn.sigmoid(preact)).astype(BF16)
-    act_x = [push(acts.at[x], zy, (x + dx) % X, lat) for dx in range(1, X)]
+    low, high = slice(0, 128), slice(128, 256)
+    act_x = [push(acts.at[x], zy, (x + dx) % X, lat) for dx in (2, 1, 3)]
 
     for copy in cot_x:
         copy.wait_recv()
@@ -305,8 +387,8 @@
         part = flat[pl.ds(q, 256, stride=4), :].astype(BF16)
         cot_grid[:, 128 * q : 128 * (q + 1)] = part
         cot_blocks[q] = part
+
     out_grad = dot(cot_grid[...], wo[...], NT).astype(BF16)
-
     for copy in act_x:
         copy.wait_recv()
     activated = jnp.concatenate([acts[s] for s in range(X)], axis=1)
@@ -335,16 +417,32 @@
 
     part_x = []
     for half_of in range(2):
-        at = slice(128 * half_of, 128 * (half_of + 1))
+        at = (low, high)[half_of]
         for dx in (2, 1, 3):
+            i = 3 * half_of + dx - 1
             to = (x + dx) % X
-            parts[dx - 1, at] = blocks[to, at].astype(BF16)
-            part_x.append(
-                push_to(parts.at[dx - 1, at], parts_in.at[dx - 1, at], zy, to, lat)
-            )
+            parts[i] = blocks[to, at].astype(BF16)
+            part_x.append(push_to(parts.at[i], parts_in.at[i], zy, to, lat))
+    preact = pre[...]
+    s = jax.nn.sigmoid(preact)
+    pre[...] = s * (1.0 + preact * (1.0 - s))
 
     def all_pres(first, start):
-        all_rows(own_pre, pres.at[1 + zy], pre_send, pre_recv, start, first, first + 8)
+        @pl.loop(first, first + 8)
+        def _(t):
+            dst = pres.at[1 + mine_of]
+            if start:
+                @pl.when(t == zy)
+                def _():
+                    pltpu.make_async_copy(own_pre.at[t], dst, pre_recv).start()
+
+            @pl.when(t != zy)
+            def _():
+                copy = remote(own_pre.at[t], dst, pre_send.at[t], pre_recv, t, x, lat)
+                if start:
+                    copy.start()
+                else:
+                    copy.wait_send()
 
         def ends(slot, to_lat):
             @pl.loop(first, first + 8)
@@ -357,26 +455,23 @@
                 else:
                     copy.wait_send()
 
-        @pl.when(zy == ZY - 1)
+        @pl.when(mine_of == ZY - 1)
         def _():
             ends(0, up)
 
-        @pl.when(zy == 0)
+        @pl.when(mine_of == 0)
         def _():
             ends(ZY + 1, down)
 
     for half_of in range(2):
-        at = slice(128 * half_of, 128 * (half_of + 1))
+        at = (low, high)[half_of]
         grad_act = blocks[x, at] + cot_blocks[x, at].astype(F32)
-        preact = pre[at]
-        s = jax.nn.sigmoid(preact)
-        slope = s * (1.0 + preact * (1.0 - s))
-        for copy in part_x[3 * half_of : 3 * half_of + 3]:
-            copy.wait_recv()
-        for i in range(X - 1):
-            grad_act = grad_act + parts_in[i, at].astype(F32)
+        for i in range(3 * half_of, 3 * half_of + 3):
+            part_x[i].wait_recv()
+        for i in range(3 * half_of, 3 * half_of + 3):
+            grad_act = grad_act + parts_in[i].astype(F32)
         own_pre[8 * half_of : 8 * (half_of + 1)] = (
-            (grad_act * slope).astype(BF16).reshape(8, 16, 128)
+            (grad_act * pre[at]).astype(BF16).reshape(8, 16, 128)
         )
         all_pres(8 * half_of, True)
 
@@ -420,7 +515,7 @@
                     mine[to, h, q, j] = piece.astype(BF16)
         for dx in (2, 1, 3):
             to = (x + dx) % X
-            sum_x.append(push_to(mine.at[to, h], sums_in.at[dx - 1, h], zy, to, lat))
+            sum_x.append(push_to(mine.at[to, h], sums_in.at[3 * h + dx - 1], zy, to, lat))
 
     rim_west = remote(
         rims.at[0], rims_in.at[x], rim_send.at[0], rim_recv.at[x],
@@ -437,7 +532,7 @@
         for copy in sum_x[3 * h : 3 * h + 3]:
             copy.wait_recv()
         for i in range(X - 1):
-            total = total + sums_in[i, h].astype(F32)
+            total = total + sums_in[3 * h + i].astype(F32)
         flat[128 * h : 128 * (h + 1), :] = total.reshape(128, 128)
 
     def add_rims(j):
@@ -468,11 +563,13 @@
     all_weights(False)
     all_rows(st, rows.at[1, zy, x], row_send, row_recv, False)
     all_rows(ct, cots.at[zy, x], cot_send, cot_recv, False)
+    middle_rows(False)
+    side_rows(False)
     all_pres(0, False)
     all_pres(8, False)
 
 
-PUSHES = 64
+PUSHES = 80
 
 
 def body(state, conv_weight, conv_bias, w_qkv, w_out, cotangent):
@@ -504,17 +601,17 @@
             pltpu.VMEM((256, 128), F32),
             pltpu.VMEM((X, 256, 128), BF16),
             pltpu.VMEM((X, 256, 128), F32),
-            pltpu.VMEM((3, 256, 128), BF16),
-            pltpu.VMEM((3, 256, 128), BF16),
+            pltpu.VMEM((6, 128, 128), BF16),
+            pltpu.VMEM((6, 128, 128), BF16),
             pltpu.VMEM((ZY, 16, 128), BF16),
             pltpu.VMEM((ZY + 2, 16, 128), BF16),
             pltpu.VMEM((256, 128), F32),
             pltpu.VMEM((X, 2, 2, 4, ZY, 128), BF16),
-            pltpu.VMEM((3, 2, 2, 4, ZY, 128), BF16),
+            pltpu.VMEM((6, 2, 4, ZY, 128), BF16),
             pltpu.VMEM((2, 2, 2, ZY, 128), BF16),
             pltpu.VMEM((X, 2, 2, ZY, 128), BF16),
             dma((8,)),
-            dma((2 * X,)),
+            dma((3 * X,)),
             dma((4,)),
             dma((ZY,)),
             dma,
@@ -525,6 +622,9 @@
             dma((ZY,)),
             dma((2,)),
             dma((X,)),
+            dma((2,)),
+            dma((2,)),
+            dma((2,)),
             dma((PUSHES,)),
             dma((PUSHES,)),
         ],

time: 71.9 us -> 71 us (0.987)
  Pallas kernels: 70.2 us -> 69.4 us
    pallas_call x1, Pallas kernels: 70.2 us -> 69.4 us  [body(): pl.pallas_call(kernel, out_shape=jax.ShapeDtypeStruct((ZY, 16, 128), BF16...]
where the time goes in v2:
time: 71 us; the launch traced here: 70.9 us
  Pallas kernels  69.4 us (98%)
  local copies, waits for them, and re-layouts  1.49 us (2%)
    pallas_call x1, Pallas kernels, body(): pl.pallas_call(kernel, out_shape=jax.ShapeDtypeStruct((ZY, 16, 128), BF16...  69.4 us
    unnamed x1, local copies, waits for them, and re-layouts  1.49 us

profile of v2, /device:TPU:64, one launch (start us, length us, event | category | flops | bytes accessed | tf_op | source)
XLA Modules:
  0.0 70.9 jit_solution(15030012559927003898)
XLA Ops:
  0.0 69.4 %shard_map.64 = bf16[16,16,128]{2,1,0:T(8,128)(2,1)} custom-call(bf16[16,4,512]{2,1,0:T(4,128)(2,1)} %st_hbm.1, bf16[16,4,512]{2,1,0:T(4,128)(2,1)} %ct_hbm.1, bf16[72,512]{1,0:T(8,128)(2,1)} %cw_hbm.1, f32[4,128]{1,0:T(4,128)} %bitcast.7, bf16[512,1536]{1,0:T(8,128)(2,1)} %wqkv.1, bf16[512,512]{1,0:T(8,128)(2,1)} %wout.1), custom_call_target="tpu_custom_call" | custom-call | tf_op jit(solution)/shard_map/pallas_call | solution.py:579
  69.4 1.5 %copy.9 = bf16[16,4,512]{2,1,0:T(4,128)(2,1)} copy(bf16[16,4,512]{2,1,0:T(4,128)(2,1)} %bitcast.6) | data formatting | bytes 131072

commit v3 on v2

--- a/solution.py
+++ b/solution.py
@@ -33,6 +33,7 @@
     raw, raw_w, st, ct, wp, bias,
     rows, cots, flat, grid, cot_grid, cot_blocks, w_one, w_all, wq, wo,
     pre, acts, blocks, parts, parts_in, own_pre, pres, shifted, mine, sums_in, rims, rims_in,
+    w_turned, wq_turned,
     load_sem, w_send, w_recv, row_send, row_recv, cot_send, cot_recv, pre_send, pre_recv,
     end_send, rim_send, rim_recv, middle_send, side_send, side_recv,
     send, recv,
@@ -302,13 +303,15 @@
         to_west.wait_recv()
         return on_east, push(east_half, zy, west, lat)
 
+    cot_load.wait()
+    relayout(1, ct)
+    all_rows(ct, cots.at[zy, x], cot_send, cot_recv, True)
+
     forward(0, 0)
     pltpu.make_async_copy(rows.at[1, :, x], rows.at[1, :, x], row_recv).wait()
     side_rows(True)
     row_x = round_x(rows.at[1, :, x], rows.at[1, 0:8, west], rows.at[1, 8:16, east])
     forward(0, 1)
-    cot_load.wait()
-    relayout(1, ct)
     forward(1, 0)
     row_on = round_x_on(*row_x)
     for i in range(2):
@@ -320,7 +323,6 @@
     above_west = push(rows.at[0, :, x], zy, west, lat)
     forward(1, 1)
     forward(2, 0)
-    all_rows(ct, cots.at[zy, x], cot_send, cot_recv, True)
     above_east.wait_recv()
     above_on = push(rows.at[0, :, west], zy, east, lat)
     below_west.wait_recv()
@@ -379,6 +381,12 @@
     acts[x] = (preact * jax.nn.sigmoid(preact)).astype(BF16)
     low, high = slice(0, 128), slice(128, 256)
     act_x = [push(acts.at[x], zy, (x + dx) % X, lat) for dx in (2, 1, 3)]
+
+    for a in range(3):
+        for b in range(3):
+            w_turned[b, 128 * a : 128 * (a + 1), :] = tap(3 * a + b).T
+    for t in range(3):
+        wq_turned[128 * t : 128 * (t + 1), :] = wq[:, 128 * t : 128 * (t + 1)].T
 
     for copy in cot_x:
         copy.wait_recv()
@@ -411,7 +419,7 @@
         ],
         axis=1,
     )
-    head_part = dot(grads, wq[...], NT)
+    head_part = dot(grads, wq_turned[...])
     for q in range(X):
         blocks[q] = head_part[:, 128 * q : 128 * (q + 1)]
 
@@ -494,8 +502,7 @@
         at = slice(256 * h, 256 * (h + 1))
         result = jnp.zeros((256, 256), F32)
         for b in range(3):
-            taps = jnp.concatenate([tap(3 * a + b)[at] for a in range(3)], axis=1)
-            acc = dot(around, taps, NT)
+            acc = dot(around, w_turned[b, :, at])
             if b != 1:
                 for q in range(2):
                     shifted[...] = acc[:, 128 * q : 128 * (q + 1)]
@@ -610,6 +617,8 @@
             pltpu.VMEM((6, 2, 4, ZY, 128), BF16),
             pltpu.VMEM((2, 2, 2, ZY, 128), BF16),
             pltpu.VMEM((X, 2, 2, ZY, 128), BF16),
+            pltpu.VMEM((3, 384, 512), BF16),
+            pltpu.VMEM((384, 512), BF16),
             dma((8,)),
             dma((3 * X,)),
             dma((4,)),

time: 71 us -> 69.1 us (0.973)
  Pallas kernels: 69.4 us -> 67.4 us
    pallas_call x1, Pallas kernels: 69.4 us -> 67.4 us  [body(): pl.pallas_call(kernel, out_shape=jax.ShapeDtypeStruct((ZY, 16, 128), BF16...]
where the time goes in v3:
time: 69.1 us; the launch traced here: 68.9 us
  Pallas kernels  67.4 us (98%)
  local copies, waits for them, and re-layouts  1.49 us (2%)
    pallas_call x1, Pallas kernels, body(): pl.pallas_call(kernel, out_shape=jax.ShapeDtypeStruct((ZY, 16, 128), BF16...  67.4 us
    unnamed x1, local copies, waits for them, and re-layouts  1.49 us

profile of v3, /device:TPU:64, one launch (start us, length us, event | category | flops | bytes accessed | tf_op | source)
XLA Modules:
  0.0 68.9 jit_solution(16887832204544717050)
XLA Ops:
  0.0 67.4 %shard_map.64 = bf16[16,16,128]{2,1,0:T(8,128)(2,1)} custom-call(bf16[16,4,512]{2,1,0:T(4,128)(2,1)} %st_hbm.1, bf16[16,4,512]{2,1,0:T(4,128)(2,1)} %ct_hbm.1, bf16[72,512]{1,0:T(8,128)(2,1)} %cw_hbm.1, f32[4,128]{1,0:T(4,128)} %bitcast.7, bf16[512,1536]{1,0:T(8,128)(2,1)} %wqkv.1, bf16[512,512]{1,0:T(8,128)(2,1)} %wout.1), custom_call_target="tpu_custom_call" | custom-call | tf_op jit(solution)/shard_map/pallas_call | solution.py:586
  67.4 1.5 %copy.9 = bf16[16,4,512]{2,1,0:T(4,128)(2,1)} copy(bf16[16,4,512]{2,1,0:T(4,128)(2,1)} %bitcast.6) | data formatting | bytes 131072

commit v4 on v3

--- a/solution.py
+++ b/solution.py
@@ -71,6 +71,13 @@
         copy.start()
         started.append(copy)
         return copy
+
+    drained = [0]
+
+    def drain():
+        for copy in started[drained[0] :]:
+            copy.wait_send()
+        drained[0] = len(started)
 
     def push(ref, to_zy, to_x, to_lat):
         return push_to(ref, ref, to_zy, to_x, to_lat)
@@ -423,6 +430,7 @@
     for q in range(X):
         blocks[q] = head_part[:, 128 * q : 128 * (q + 1)]
 
+    early = len(started)
     part_x = []
     for half_of in range(2):
         at = (low, high)[half_of]
@@ -434,6 +442,14 @@
     preact = pre[...]
     s = jax.nn.sigmoid(preact)
     pre[...] = s * (1.0 + preact * (1.0 - s))
+    for copy in started[:early]:
+        copy.wait_send()
+    drained[0] = early
+    all_weights(False)
+    all_rows(st, rows.at[1, zy, x], row_send, row_recv, False)
+    all_rows(ct, cots.at[zy, x], cot_send, cot_recv, False)
+    middle_rows(False)
+    side_rows(False)
 
     def all_pres(first, start):
         @pl.loop(first, first + 8)
@@ -483,6 +499,7 @@
         )
         all_pres(8 * half_of, True)
 
+    drain()
     pltpu.make_async_copy(pres, pres, pre_recv).wait()
 
     @pl.when(lat == 0)
@@ -533,6 +550,8 @@
     )
     rim_west.start()
     rim_east.start()
+    all_pres(0, False)
+    all_pres(8, False)
 
     for h in range(2):
         total = mine[x, h].astype(F32)
@@ -565,15 +584,7 @@
 
     rim_west.wait_send()
     rim_east.wait_send()
-    for copy in started:
-        copy.wait_send()
-    all_weights(False)
-    all_rows(st, rows.at[1, zy, x], row_send, row_recv, False)
-    all_rows(ct, cots.at[zy, x], cot_send, cot_recv, False)
-    middle_rows(False)
-    side_rows(False)
-    all_pres(0, False)
-    all_pres(8, False)
+    drain()
 
 
 PUSHES = 80

time: 69.1 us -> 68.4 us (0.990)
  no operation moved by 1% of the time
where the time goes in v4:
time: 68.4 us; the launch traced here: 68.3 us
  Pallas kernels  66.8 us (98%)
  local copies, waits for them, and re-layouts  1.49 us (2%)
    pallas_call x1, Pallas kernels, body(): pl.pallas_call(kernel, out_shape=jax.ShapeDtypeStruct((ZY, 16, 128), BF16...  66.8 us
    unnamed x1, local copies, waits for them, and re-layouts  1.49 us

profile of v4, /device:TPU:64, one launch (start us, length us, event | category | flops | bytes accessed | tf_op | source)
XLA Modules:
  0.0 68.3 jit_solution(18111894965844874579)
XLA Ops:
  0.0 66.8 %shard_map.64 = bf16[16,16,128]{2,1,0:T(8,128)(2,1)} custom-call(bf16[16,4,512]{2,1,0:T(4,128)(2,1)} %st_hbm.1, bf16[16,4,512]{2,1,0:T(4,128)(2,1)} %ct_hbm.1, bf16[72,512]{1,0:T(8,128)(2,1)} %cw_hbm.1, f32[4,128]{1,0:T(4,128)} %bitcast.7, bf16[512,1536]{1,0:T(8,128)(2,1)} %wqkv.1, bf16[512,512]{1,0:T(8,128)(2,1)} %wout.1), custom_call_target="tpu_custom_call" | custom-call | tf_op jit(solution)/shard_map/pallas_call | solution.py:597
  66.8 1.5 %copy.9 = bf16[16,4,512]{2,1,0:T(4,128)(2,1)} copy(bf16[16,4,512]{2,1,0:T(4,128)(2,1)} %bitcast.6) | data formatting | bytes 131072

commit v5 on v4

--- a/solution.py
+++ b/solution.py
@@ -32,7 +32,7 @@
     st_hbm, ct_hbm, cw_hbm, bias_hbm, wqkv, wout, out,
     raw, raw_w, st, ct, wp, bias,
     rows, cots, flat, grid, cot_grid, cot_blocks, w_one, w_all, wq, wo,
-    pre, acts, blocks, parts, parts_in, own_pre, pres, shifted, mine, sums_in, rims, rims_in,
+    pre, acts, blocks, parts, parts_in, own_pre, pres, mine, sums_in, rims, rims_in,
     w_turned, wq_turned,
     load_sem, w_send, w_recv, row_send, row_recv, cot_send, cot_recv, pre_send, pre_recv,
     end_send, rim_send, rim_recv, middle_send, side_send, side_recv,
@@ -198,9 +198,13 @@
     state_load.wait()
     relayout(0, st)
 
+    lead = jnp.where(z == core, Y, 0)
+
     def all_rows(src, dst, send_sem, recv_sem, start):
         @pl.loop(0, ZY)
-        def _(t):
+        def _(i):
+            t = (i + lead) % ZY
+
             if start:
                 @pl.when(t == mine_of)
                 def _():
@@ -386,7 +390,6 @@
     )
     pre[...] = preact
     acts[x] = (preact * jax.nn.sigmoid(preact)).astype(BF16)
-    low, high = slice(0, 128), slice(128, 256)
     act_x = [push(acts.at[x], zy, (x + dx) % X, lat) for dx in (2, 1, 3)]
 
     for a in range(3):
@@ -432,8 +435,10 @@
 
     early = len(started)
     part_x = []
+    sides = (1 - z, z)
+    halves = [pl.ds(pl.multiple_of(side * 128, 128), 128) for side in sides]
     for half_of in range(2):
-        at = (low, high)[half_of]
+        at = halves[half_of]
         for dx in (2, 1, 3):
             i = 3 * half_of + dx - 1
             to = (x + dx) % X
@@ -488,16 +493,17 @@
             ends(ZY + 1, down)
 
     for half_of in range(2):
-        at = (low, high)[half_of]
+        at = halves[half_of]
+        first = 8 * sides[half_of]
         grad_act = blocks[x, at] + cot_blocks[x, at].astype(F32)
         for i in range(3 * half_of, 3 * half_of + 3):
             part_x[i].wait_recv()
         for i in range(3 * half_of, 3 * half_of + 3):
             grad_act = grad_act + parts_in[i].astype(F32)
-        own_pre[8 * half_of : 8 * (half_of + 1)] = (
+        own_pre[pl.ds(first, 8)] = (
             (grad_act * pre[at]).astype(BF16).reshape(8, 16, 128)
         )
-        all_pres(8 * half_of, True)
+        all_pres(first, True)
 
     drain()
     pltpu.make_async_copy(pres, pres, pre_recv).wait()
@@ -513,6 +519,23 @@
     around = jnp.concatenate(
         [pres[2 - a : 2 - a + ZY].reshape(256, 128) for a in range(3)], axis=1
     )
+
+    flat[0:288, :] = pres[...].reshape(288, 128).astype(F32)
+    for side, b, at in ((0, 0, 0), (1, 2, 15)):
+        edge_of = [flat[pl.ds(16 * (2 - a) + at, 16, stride=16), :] for a in range(3)]
+        rim = dot(jnp.concatenate(edge_of, axis=1).astype(BF16), w_turned[b])
+        for q in range(4):
+            rims[side, q // 2, q % 2] = rim[:, 128 * q : 128 * (q + 1)].astype(BF16)
+    rim_west = remote(
+        rims.at[0], rims_in.at[x], rim_send.at[0], rim_recv.at[x],
+        (zy + ZY - 1) % ZY, X - 1, lat,
+    )
+    rim_east = remote(
+        rims.at[1], rims_in.at[x], rim_send.at[1], rim_recv.at[x], (zy + 1) % ZY, 0, lat
+    )
+    rim_west.start()
+    rim_east.start()
+
     column = lax.broadcasted_iota(jnp.int32, (256, 256), 0) % 16
     sum_x = []
     for h in range(2):
@@ -520,11 +543,6 @@
         result = jnp.zeros((256, 256), F32)
         for b in range(3):
             acc = dot(around, w_turned[b, :, at])
-            if b != 1:
-                for q in range(2):
-                    shifted[...] = acc[:, 128 * q : 128 * (q + 1)]
-                    rim = shifted[pl.ds(0 if b == 0 else 15, 16, stride=16), :]
-                    rims[b // 2, h, q] = rim.astype(BF16)
             if b == 0:
                 acc = jnp.where(column == 15, 0.0, pltpu.roll(acc, 255, 0))
             if b == 2:
@@ -541,15 +559,6 @@
             to = (x + dx) % X
             sum_x.append(push_to(mine.at[to, h], sums_in.at[3 * h + dx - 1], zy, to, lat))
 
-    rim_west = remote(
-        rims.at[0], rims_in.at[x], rim_send.at[0], rim_recv.at[x],
-        (zy + ZY - 1) % ZY, X - 1, lat,
-    )
-    rim_east = remote(
-        rims.at[1], rims_in.at[x], rim_send.at[1], rim_recv.at[x], (zy + 1) % ZY, 0, lat
-    )
-    rim_west.start()
-    rim_east.start()
     all_pres(0, False)
     all_pres(8, False)
 
@@ -623,7 +632,6 @@
             pltpu.VMEM((6, 128, 128), BF16),
             pltpu.VMEM((ZY, 16, 128), BF16),
             pltpu.VMEM((ZY + 2, 16, 128), BF16),
-            pltpu.VMEM((256, 128), F32),
             pltpu.VMEM((X, 2, 2, 4, ZY, 128), BF16),
             pltpu.VMEM((6, 2, 4, ZY, 128), BF16),
             pltpu.VMEM((2, 2, 2, ZY, 128), BF16),

time: 68.4 us -> 67.1 us (0.981)
  Pallas kernels: 66.8 us -> 65.5 us
    pallas_call x1, Pallas kernels: 66.8 us -> 65.5 us  [body(): pl.pallas_call(kernel, out_shape=jax.ShapeDtypeStruct((ZY, 16, 128), BF16...]
where the time goes in v5:
time: 67.1 us; the launch traced here: 67 us
  Pallas kernels  65.5 us (98%)
  local copies, waits for them, and re-layouts  1.49 us (2%)
    pallas_call x1, Pallas kernels, body(): pl.pallas_call(kernel, out_shape=jax.ShapeDtypeStruct((ZY, 16, 128), BF16...  65.5 us
    unnamed x1, local copies, waits for them, and re-layouts  1.49 us

profile of v5, /device:TPU:64, one launch (start us, length us, event | category | flops | bytes accessed | tf_op | source)
XLA Modules:
  0.0 67.0 jit_solution(13915501386040720571)
XLA Ops:
  0.0 65.5 %shard_map.64 = bf16[16,16,128]{2,1,0:T(8,128)(2,1)} custom-call(bf16[16,4,512]{2,1,0:T(4,128)(2,1)} %st_hbm.1, bf16[16,4,512]{2,1,0:T(4,128)(2,1)} %ct_hbm.1, bf16[72,512]{1,0:T(8,128)(2,1)} %cw_hbm.1, f32[4,128]{1,0:T(4,128)} %bitcast.7, bf16[512,1536]{1,0:T(8,128)(2,1)} %wqkv.1, bf16[512,512]{1,0:T(8,128)(2,1)} %wout.1), custom_call_target="tpu_custom_call" | custom-call | tf_op jit(solution)/shard_map/pallas_call | solution.py:606
  65.5 1.5 %copy.9 = bf16[16,4,512]{2,1,0:T(4,128)(2,1)} copy(bf16[16,4,512]{2,1,0:T(4,128)(2,1)} %bitcast.6) | data formatting | bytes 131072

commit v6 on v5

--- a/solution.py
+++ b/solution.py
@@ -269,36 +269,41 @@
             both.append(w_one[2 * part + i].astype(F32)[:72])
         w_all[part, half(y, core), :] = jnp.concatenate(both, axis=0).astype(BF16)
 
-    right = z * Y + (y + 1) % Y
-    left = z * Y + (y + Y - 1) % Y
-
-    def ring(turn, place, to):
+    def along(turn, place, step):
+        to = z * Y + (y + Y + step) % Y
         return push(w_all.at[(z, 1 - z)[turn], half(place, core)], to, x, lat)
 
-    rights = [[]]
-    lefts = [[]]
     pair = []
-    for turn in range(2):
-        take_weight((z, 1 - z)[turn])
-        rights[0].append(ring(turn, y, right))
-        lefts[0].append(ring(turn, y, left))
-        pair.append(push(w_all.at[(z, 1 - z)[turn], half(y, core)], zy, x, sib))
-
-    def forward(step, turn):
-        turns = (
-            (rights, right, (y + Y - 1 - step) % Y, 0),
-            (lefts, left, (y + 1 + step) % Y, 1),
-        )
-        for copies, to, got, last in turns:
-            if turn == 0:
-                copies.append([None, None])
-            copy = copies[step][turn]
-            if copy is None:
-                continue
-            copy.wait_recv()
-            if step < 2 or (step == 2 and turn == last):
-                copies[step + 1][turn] = ring(turn, got, to)
-            pair.append(push(w_all.at[(z, 1 - z)[turn], half(got, core)], zy, x, sib))
+
+    def to_pair(turn, place):
+        pair.append(push(w_all.at[(z, 1 - z)[turn], half(place, core)], zy, x, sib))
+
+    take_weight(z)
+    rights, lefts = [along(0, y, 1)], [along(0, y, -1)]
+    to_pair(0, y)
+    take_weight(1 - z)
+    nearest = [along(1, y, step) for step in (1, -1, 2, -2)]
+    to_pair(1, y)
+
+    def forward(step):
+        for copies, way, steps in ((rights, 1, 4), (lefts, -1, 3)):
+            if step < steps:
+                copies[step].wait_recv()
+                place = (y + Y - way * (step + 1)) % Y
+                if step + 1 < steps:
+                    copies.append(along(0, place, way))
+                to_pair(0, place)
+
+    handed = []
+
+    def hand_on(which, on):
+        step = (1, -1, 2, -2)[which]
+        nearest[which].wait_recv()
+        place = (y + Y - step) % Y
+        if on:
+            by = 2 if step > 0 else -2
+            handed.append((along(1, place, by), (y + Y - step - by) % Y))
+        to_pair(1, place)
 
     def round_x(whole, west_half, east_half):
         return (
@@ -318,27 +323,27 @@
     relayout(1, ct)
     all_rows(ct, cots.at[zy, x], cot_send, cot_recv, True)
 
-    forward(0, 0)
+    forward(0)
     pltpu.make_async_copy(rows.at[1, :, x], rows.at[1, :, x], row_recv).wait()
     side_rows(True)
     row_x = round_x(rows.at[1, :, x], rows.at[1, 0:8, west], rows.at[1, 8:16, east])
-    forward(0, 1)
-    forward(1, 0)
+    hand_on(0, True)
+    hand_on(1, True)
+    forward(1)
+    hand_on(2, False)
+    hand_on(3, True)
     row_on = round_x_on(*row_x)
     for i in range(2):
         at = rows.at[2 * i, :, x]
         pltpu.make_async_copy(at, at, side_recv.at[i]).wait()
-    above_east = push(rows.at[0, :, x], zy, east, lat)
-    below_west = push(rows.at[2, :, x], zy, west, lat)
-    below_east = push(rows.at[2, :, x], zy, east, lat)
-    above_west = push(rows.at[0, :, x], zy, west, lat)
-    forward(1, 1)
-    forward(2, 0)
-    above_east.wait_recv()
-    above_on = push(rows.at[0, :, west], zy, east, lat)
-    below_west.wait_recv()
-    below_on = push(rows.at[2, :, east], zy, west, lat)
-    forward(2, 1)
+    side_x = [
+        [push(rows.at[2 * i, :, x], zy, (x + dx) % X, lat) for i in range(2)]
+        for dx in (2, 1, 3)
+    ]
+    forward(2)
+    for copy, place in handed:
+        copy.wait_recv()
+        to_pair(1, place)
 
     def whole_row(a):
         flat[...] = rows[a].reshape(1024, 128).astype(F32)
@@ -353,18 +358,16 @@
     for copy in row_on:
         copy.wait_recv()
     whole_row(1)
-    forward(3, 0)
-    forward(3, 1)
 
     pltpu.make_async_copy(cots.at[:, x], cots.at[:, x], cot_recv).wait()
     cot_x = [push(cots.at[:, x], zy, (x + dx) % X, lat) for dx in range(1, X)]
 
-    below_east.wait_recv()
-    above_west.wait_recv()
-    above_on.wait_recv()
-    whole_row(0)
-    below_on.wait_recv()
-    whole_row(2)
+    forward(3)
+
+    for i in range(2):
+        for copies in side_x:
+            copies[i].wait_recv()
+        whole_row(2 * i)
     for copy in loads:
         copy.wait()
     for copy in pair:

time: 67.1 us -> 67 us (level)
  no operation moved by 1% of the time
where the time goes in v6:
time: 67 us; the launch traced here: 66.8 us
  Pallas kernels  65.3 us (97%)
  local copies, waits for them, and re-layouts  1.49 us (2%)
    pallas_call x1, Pallas kernels, body(): pl.pallas_call(kernel, out_shape=jax.ShapeDtypeStruct((ZY, 16, 128), BF16...  65.3 us
    unnamed x1, local copies, waits for them, and re-layouts  1.49 us

profile of v6, /device:TPU:64, one launch (start us, length us, event | category | flops | bytes accessed | tf_op | source)
XLA Modules:
  0.0 66.8 jit_solution(14433761379752994053)
XLA Ops:
  0.0 65.3 %shard_map.64 = bf16[16,16,128]{2,1,0:T(8,128)(2,1)} custom-call(bf16[16,4,512]{2,1,0:T(4,128)(2,1)} %st_hbm.1, bf16[16,4,512]{2,1,0:T(4,128)(2,1)} %ct_hbm.1, bf16[72,512]{1,0:T(8,128)(2,1)} %cw_hbm.1, f32[4,128]{1,0:T(4,128)} %bitcast.7, bf16[512,1536]{1,0:T(8,128)(2,1)} %wqkv.1, bf16[512,512]{1,0:T(8,128)(2,1)} %wout.1), custom_call_target="tpu_custom_call" | custom-call | tf_op jit(solution)/shard_map/pallas_call | solution.py:609
  65.3 1.5 %copy.9 = bf16[16,4,512]{2,1,0:T(4,128)(2,1)} copy(bf16[16,4,512]{2,1,0:T(4,128)(2,1)} %bitcast.6) | data formatting | bytes 131072

commit v7 on v6

--- a/solution.py
+++ b/solution.py
@@ -90,12 +90,6 @@
     weight_load = load(0, cw_hbm, raw_w)
     state_load = load(1, st_hbm, raw.at[0])
     cot_load = load(2, ct_hbm, raw.at[1])
-    loads = [load(3, bias_hbm, bias)]
-    for t in range(3):
-        source = wqkv.at[:, pl.ds(pl.multiple_of(t * 512 + x * 128, 128), 128)]
-        loads.append(load(4 + t, source, wq.at[:, 128 * t : 128 * (t + 1)]))
-    loads.append(load(7, wout.at[pl.ds(pl.multiple_of(x * 128, 128), 128)], wo))
-
     barrier = pltpu.get_barrier_semaphore()
 
     def hello(to_zy, to_x, to_lat):
@@ -132,6 +126,12 @@
     def _():
         for i in range(X):
             hello((zy + 1) % ZY, i, lat)
+
+    loads = [load(3, bias_hbm, bias)]
+    for t in range(3):
+        source = wqkv.at[:, pl.ds(pl.multiple_of(t * 512 + x * 128, 128), 128)]
+        loads.append(load(4 + t, source, wq.at[:, 128 * t : 128 * (t + 1)]))
+    loads.append(load(7, wout.at[pl.ds(pl.multiple_of(x * 128, 128), 128)], wo))
 
     weight_load.wait()
     for q in range(X):
@@ -364,10 +364,6 @@
 
     forward(3)
 
-    for i in range(2):
-        for copies in side_x:
-            copies[i].wait_recv()
-        whole_row(2 * i)
     for copy in loads:
         copy.wait()
     for copy in pair:
@@ -383,6 +379,10 @@
     two = jnp.zeros((256, 256), F32)
     third = jnp.zeros((256, 128), F32)
     for a in (1, 0, 2):
+        if a != 1:
+            for copies in side_x:
+                copies[a // 2].wait_recv()
+            whole_row(a)
         two = two + dot(grid[a], jnp.concatenate([tap(3 * a), tap(3 * a + 1)], axis=1))
         third = third + dot(grid[a], tap(3 * a + 2))
     preact = (
@@ -417,7 +417,7 @@
     queries, keys, values = (projected[:, 128 * t : 128 * (t + 1)] for t in range(3))
     capped = jnp.tanh(dot(queries, keys, NT) * (INV_ROOT / CAP))
     expo = jnp.exp(CAP * capped)
-    probs = expo / jnp.sum(expo, axis=-1, keepdims=True)
+    probs = expo * (1.0 / jnp.sum(expo, axis=-1, keepdims=True))
     probs_b = probs.astype(BF16)
     attended = dot(probs_b, values).astype(BF16)
     centre = jnp.sum(out_grad.astype(F32) * attended.astype(F32), axis=-1, keepdims=True)

time: 67 us -> 66.6 us (level)
  no operation moved by 1% of the time
where the time goes in v7:
time: 66.6 us; the launch traced here: 66.4 us
  Pallas kernels  64.9 us (97%)
  local copies, waits for them, and re-layouts  1.49 us (2%)
    pallas_call x1, Pallas kernels, body(): pl.pallas_call(kernel, out_shape=jax.ShapeDtypeStruct((ZY, 16, 128), BF16...  64.9 us
    unnamed x1, local copies, waits for them, and re-layouts  1.49 us

profile of v7, /device:TPU:64, one launch (start us, length us, event | category | flops | bytes accessed | tf_op | source)
XLA Modules:
  0.0 66.4 jit_solution(15802095114600119881)
XLA Ops:
  0.0 64.9 %shard_map.64 = bf16[16,16,128]{2,1,0:T(8,128)(2,1)} custom-call(bf16[16,4,512]{2,1,0:T(4,128)(2,1)} %st_hbm.1, bf16[16,4,512]{2,1,0:T(4,128)(2,1)} %ct_hbm.1, bf16[72,512]{1,0:T(8,128)(2,1)} %cw_hbm.1, f32[4,128]{1,0:T(4,128)} %bitcast.7, bf16[512,1536]{1,0:T(8,128)(2,1)} %wqkv.1, bf16[512,512]{1,0:T(8,128)(2,1)} %wout.1), custom_call_target="tpu_custom_call" | custom-call | tf_op jit(solution)/shard_map/pallas_call | solution.py:609
  64.9 1.5 %copy.9 = bf16[16,4,512]{2,1,0:T(4,128)(2,1)} copy(bf16[16,4,512]{2,1,0:T(4,128)(2,1)} %bitcast.6) | data formatting | bytes 131072

commit v8 on v7

--- a/solution.py
+++ b/solution.py
@@ -198,27 +198,23 @@
     state_load.wait()
     relayout(0, st)
 
-    lead = jnp.where(z == core, Y, 0)
+    across_z = [(1 - z) * Y + (y + k) % Y for k in range(Y)]
+    along_y = [z * Y + (y + k) % Y for k in range(1, Y)]
+
+    def row_of(place):
+        return jnp.where(place // Y == core, place % Y, ZY - 1 - place % Y)
 
     def all_rows(src, dst, send_sem, recv_sem, start):
-        @pl.loop(0, ZY)
-        def _(i):
-            t = (i + lead) % ZY
-
+        for k, place in enumerate(across_z + along_y):
+            copy = remote(
+                src.at[row_of(place)], dst, send_sem.at[k], recv_sem, place, x, lat
+            )
             if start:
-                @pl.when(t == mine_of)
-                def _():
-                    pltpu.make_async_copy(src.at[t], dst, recv_sem).start()
-
-            @pl.when(t != mine_of)
-            def _():
-                copy = remote(
-                    src.at[t], dst, send_sem.at[t], recv_sem, owner(t), x, lat
-                )
-                if start:
-                    copy.start()
-                else:
-                    copy.wait_send()
+                copy.start()
+            else:
+                copy.wait_send()
+        if start:
+            pltpu.make_async_copy(src.at[mine_of], dst, recv_sem).start()
 
     def middle_rows(start):
         for i, t, to in ((0, Y - 1, Y), (1, Y, Y - 1)):
@@ -459,33 +455,25 @@
     middle_rows(False)
     side_rows(False)
 
-    def all_pres(first, start):
-        @pl.loop(first, first + 8)
-        def _(t):
-            dst = pres.at[1 + mine_of]
-            if start:
-                @pl.when(t == zy)
-                def _():
-                    pltpu.make_async_copy(own_pre.at[t], dst, pre_recv).start()
-
-            @pl.when(t != zy)
-            def _():
-                copy = remote(own_pre.at[t], dst, pre_send.at[t], pre_recv, t, x, lat)
-                if start:
-                    copy.start()
-                else:
-                    copy.wait_send()
-
-        def ends(slot, to_lat):
-            @pl.loop(first, first + 8)
-            def _(t):
+    def all_pres(half_of, start):
+        def send_all(places, slot, sems, base, to_lat):
+            for k, place in enumerate(places):
                 copy = remote(
-                    own_pre.at[t], pres.at[slot], end_send.at[t], pre_recv, t, x, to_lat
+                    own_pre.at[place], pres.at[slot], sems.at[base + k], pre_recv,
+                    place, x, to_lat,
                 )
                 if start:
                     copy.start()
                 else:
                     copy.wait_send()
+
+        def ends(slot, to_lat):
+            places = along_y + [zy] if half_of else across_z
+            send_all(places, slot, end_send, Y * half_of, to_lat)
+
+        send_all((across_z, along_y)[half_of], 1 + mine_of, pre_send, Y * half_of, lat)
+        if start and half_of:
+            pltpu.make_async_copy(own_pre.at[zy], pres.at[1 + mine_of], pre_recv).start()
 
         @pl.when(mine_of == ZY - 1)
         def _():
@@ -506,7 +494,7 @@
         own_pre[pl.ds(first, 8)] = (
             (grad_act * pre[at]).astype(BF16).reshape(8, 16, 128)
         )
-        all_pres(first, True)
+        all_pres(half_of, True)
 
     drain()
     pltpu.make_async_copy(pres, pres, pre_recv).wait()
@@ -563,7 +551,7 @@
             sum_x.append(push_to(mine.at[to, h], sums_in.at[3 * h + dx - 1], zy, to, lat))
 
     all_pres(0, False)
-    all_pres(8, False)
+    all_pres(1, False)
 
     for h in range(2):
         total = mine[x, h].astype(F32)

time: 66.6 us -> 66.9 us (level)
  no operation moved by 1% of the time
where the time goes in v8:
time: 66.9 us; the launch traced here: 66.7 us
  Pallas kernels  65.2 us (97%)
  local copies, waits for them, and re-layouts  1.49 us (2%)
    pallas_call x1, Pallas kernels, body(): pl.pallas_call(kernel, out_shape=jax.ShapeDtypeStruct((ZY, 16, 128), BF16...  65.2 us
    unnamed x1, local copies, waits for them, and re-layouts  1.49 us

profile of v8, /device:TPU:64, one launch (start us, length us, event | category | flops | bytes accessed | tf_op | source)
XLA Modules:
  0.0 66.7 jit_solution(18046984280023446173)
XLA Ops:
  0.0 65.2 %shard_map.64 = bf16[16,16,128]{2,1,0:T(8,128)(2,1)} custom-call(bf16[16,4,512]{2,1,0:T(4,128)(2,1)} %st_hbm.1, bf16[16,4,512]{2,1,0:T(4,128)(2,1)} %ct_hbm.1, bf16[72,512]{1,0:T(8,128)(2,1)} %cw_hbm.1, f32[4,128]{1,0:T(4,128)} %bitcast.7, bf16[512,1536]{1,0:T(8,128)(2,1)} %wqkv.1, bf16[512,512]{1,0:T(8,128)(2,1)} %wout.1), custom_call_target="tpu_custom_call" | custom-call | tf_op jit(solution)/shard_map/pallas_call | solution.py:597
  65.2 1.5 %copy.9 = bf16[16,4,512]{2,1,0:T(4,128)(2,1)} copy(bf16[16,4,512]{2,1,0:T(4,128)(2,1)} %bitcast.6) | data formatting | bytes 131072

commit v9 on v7

--- a/solution.py
+++ b/solution.py
@@ -341,6 +341,8 @@
         for dx in (2, 1, 3)
     ]
     forward(2)
+    pltpu.make_async_copy(cots.at[:, x], cots.at[:, x], cot_recv).wait()
+    cot_x = [push(cots.at[:, x], zy, (x + dx) % X, lat) for dx in range(1, X)]
     for copy, place in handed:
         copy.wait_recv()
         to_pair(1, place)
@@ -358,9 +360,6 @@
     for copy in row_on:
         copy.wait_recv()
     whole_row(1)
-
-    pltpu.make_async_copy(cots.at[:, x], cots.at[:, x], cot_recv).wait()
-    cot_x = [push(cots.at[:, x], zy, (x + dx) % X, lat) for dx in range(1, X)]
 
     forward(3)
 

time: 66.6 us -> 66.8 us (level)
  no operation moved by 1% of the time
where the time goes in v9:
time: 66.8 us; the launch traced here: 66.6 us
  Pallas kernels  65.1 us (97%)
  local copies, waits for them, and re-layouts  1.49 us (2%)
    pallas_call x1, Pallas kernels, body(): pl.pallas_call(kernel, out_shape=jax.ShapeDtypeStruct((ZY, 16, 128), BF16...  65.1 us
    unnamed x1, local copies, waits for them, and re-layouts  1.49 us

profile of v9, /device:TPU:64, one launch (start us, length us, event | category | flops | bytes accessed | tf_op | source)
XLA Modules:
  0.0 66.6 jit_solution(17802464597807602956)
XLA Ops:
  0.0 65.1 %shard_map.64 = bf16[16,16,128]{2,1,0:T(8,128)(2,1)} custom-call(bf16[16,4,512]{2,1,0:T(4,128)(2,1)} %st_hbm.1, bf16[16,4,512]{2,1,0:T(4,128)(2,1)} %ct_hbm.1, bf16[72,512]{1,0:T(8,128)(2,1)} %cw_hbm.1, f32[4,128]{1,0:T(4,128)} %bitcast.7, bf16[512,1536]{1,0:T(8,128)(2,1)} %wqkv.1, bf16[512,512]{1,0:T(8,128)(2,1)} %wout.1), custom_call_target="tpu_custom_call" | custom-call | tf_op jit(solution)/shard_map/pallas_call | solution.py:608
  65.1 1.5 %copy.9 = bf16[16,4,512]{2,1,0:T(4,128)(2,1)} copy(bf16[16,4,512]{2,1,0:T(4,128)(2,1)} %bitcast.6) | data formatting | bytes 131072
